TPU v7x, 32 devices: a whole 2x2x4 slice. The times are simulated.
32 devices in a mesh: grp: 8 (over z, core), blk: 4 (over y, x).
Axes of the slice: x: 2, y: 2, z: 4, core: 2. Of those that a mesh axis runs over, the one named last changes fastest.
Arguments:
- temp: float32 [8, 512, 512], P(None, 'grp', 'blk'), may hold values from -6 to 6
- uvel: float32 [8, 512, 512], P(None, 'grp', 'blk'), may hold values from -0.4 to 0.4
- vvel: float32 [8, 512, 512], P(None, 'grp', 'blk'), may hold values from -0.4 to 0.4
- couple_col: int32 [8, 4, 2048], P('grp', 'blk'), may hold values from 0 to 8191
- couple_cell: int32 [8, 4, 2048], P('grp', 'blk'), may hold values from 0 to 524287
- cavity: int32 [8, 4, 2048], P('grp', 'blk'), may hold values 0 or 1
- thickness: float32 [512, 1024], P('blk'), may hold values from 0.2 to 2
- viscosity: float32 [512, 1024], P('blk'), may hold values from 0.5 to 4
- friction: float32 [512, 1024], P('blk'), may hold values from 0.02 to 0.3
- drive: float32 [512, 1024], P('blk'), may hold values from -6 to 6
Outputs:
- temp_new: float32 [8, 512, 512], P(None, 'grp', 'blk')
- ice_velocity: float32 [512, 1024], P('blk')
Inputs may be any that keep to these rules, and one draw needn't show every extreme that they name: `couple_col`: an index of a column within the 64 x 128 block of the device holding the entry, row-major. `couple_cell`: a row-major index into the whole ice grid.
All inputs are finite; a program needn't handle non-finite values. No bound on the sum of `cavity` on one device may be relied on, other than what follows from the above.
Results may differ from a plain program's by a relative error of at most 0.0003.
Values sent between devices are 32-bit elements; how exact they have to be, the bound alone decides.
A program may use at most 64 MiB of HBM per device.

v0:
```python
import jax
import jax.numpy as jnp
from jax import lax
from jax.sharding import PartitionSpec as P

LEVELS = 3
SMOOTH_SWEEPS = 2
COARSE_SWEEPS = 4
CYCLES = 2


omega = 0.8
kappa = 0.1
vertical_mix = 0.2
melt_rate = 0.5


def with_halo(block, sides, width):
    for axis, dim in sides:
        count = lax.axis_size(axis)
        forward = [(i, i + 1) for i in range(count - 1)]
        backward = [(target, source) for source, target in forward]
        low = lax.ppermute(
            lax.slice_in_dim(block, block.shape[dim] - width, None, axis=dim), axis, forward
        )
        high = lax.ppermute(lax.slice_in_dim(block, 0, width, axis=dim), axis, backward)
        block = jnp.concatenate([low, block, high], axis=dim)
    return block


def face_terms(visc_pad, friction, scale):
    center = visc_pad[1:-1, 1:-1]
    east = 0.5 * (center + visc_pad[2:, 1:-1]) * scale
    west = 0.5 * (center + visc_pad[:-2, 1:-1]) * scale
    north = 0.5 * (center + visc_pad[1:-1, 2:]) * scale
    south = 0.5 * (center + visc_pad[1:-1, :-2]) * scale
    diagonal = east + west + north + south + friction
    return (east, west, north, south, diagonal)


def apply_padded(field_pad, terms):
    east, west, north, south, diagonal = terms
    field = field_pad[1:-1, 1:-1]
    return (
        diagonal * field
        - east * field_pad[2:, 1:-1]
        - west * field_pad[:-2, 1:-1]
        - north * field_pad[1:-1, 2:]
        - south * field_pad[1:-1, :-2]
    )


def restrict(field):
    paired = field[0::2] + field[1::2]
    return 0.25 * (paired[:, 0::2] + paired[:, 1::2])


def prolong(field):
    rows, cols = field.shape
    expand = (jnp.arange(2 * cols)[None, :] // 2 == jnp.arange(cols)[:, None]).astype(jnp.float32)
    wide = jnp.dot(field, expand, precision=lax.Precision.HIGHEST)
    return jnp.broadcast_to(wide[:, None, :], (rows, 2, 2 * cols)).reshape(2 * rows, 2 * cols)


def vcycle(depth, field, source, terms_list, operate):
    terms = terms_list[depth]
    sweeps = COARSE_SWEEPS if depth == LEVELS - 1 else SMOOTH_SWEEPS
    for sweep_index in range(sweeps):
        field = field + omega * (source - operate(field, terms)) / terms[4]
    if depth == LEVELS - 1:
        return field
    residual = source - operate(field, terms)
    coarse_source = restrict(residual)
    coarse = vcycle(depth + 1, jnp.zeros_like(coarse_source), coarse_source, terms_list, operate)
    field = field + prolong(coarse)
    for sweep_index in range(SMOOTH_SWEEPS):
        field = field + omega * (source - operate(field, terms)) / terms[4]
    return field


def ocean_tendency(temp_pad, uvel_pad, vvel_pad):
    temp = temp_pad[:, 1:-1, 1:-1]
    uvel = uvel_pad[:, 1:-1, 1:-1]
    vvel = vvel_pad[:, 1:-1, 1:-1]
    east_speed = 0.5 * (uvel + uvel_pad[:, 2:, 1:-1])
    flux_east = (
        jnp.maximum(east_speed, 0.0) * temp + jnp.minimum(east_speed, 0.0) * temp_pad[:, 2:, 1:-1]
    )
    west_speed = 0.5 * (uvel + uvel_pad[:, :-2, 1:-1])
    flux_west = (
        jnp.maximum(west_speed, 0.0) * temp_pad[:, :-2, 1:-1] + jnp.minimum(west_speed, 0.0) * temp
    )
    north_speed = 0.5 * (vvel + vvel_pad[:, 1:-1, 2:])
    flux_north = (
        jnp.maximum(north_speed, 0.0) * temp + jnp.minimum(north_speed, 0.0) * temp_pad[:, 1:-1, 2:]
    )
    south_speed = 0.5 * (vvel + vvel_pad[:, 1:-1, :-2])
    flux_south = (
        jnp.maximum(south_speed, 0.0) * temp_pad[:, 1:-1, :-2]
        + jnp.minimum(south_speed, 0.0) * temp
    )
    laplace = (
        temp_pad[:, 2:, 1:-1]
        + temp_pad[:, :-2, 1:-1]
        + temp_pad[:, 1:-1, 2:]
        + temp_pad[:, 1:-1, :-2]
        - 4.0 * temp
    )
    between = temp[1:] - temp[:-1]
    zero_layer = jnp.zeros_like(temp[:1])
    vert = jnp.concatenate([between, zero_layer], axis=0) - jnp.concatenate(
        [zero_layer, between], axis=0
    )
    return (
        temp
        + flux_west
        - flux_east
        + flux_south
        - flux_north
        + kappa * laplace
        + vertical_mix * vert
    )


def cells_halo(field):
    return with_halo(field, (("blk", 0),), 1)


def coeffs_halo(field):
    return with_halo(field, (("blk", 0),), 1)


def level_terms(viscosity, friction, extend):
    terms_list = []
    visc = viscosity
    fric = friction
    for depth in range(LEVELS):
        visc_halo = extend(visc)
        terms_list.append(face_terms(jnp.pad(visc_halo, ((0, 0), (1, 1))), fric, 0.25**depth))
        if depth + 1 < LEVELS:
            visc = restrict(visc)
            fric = restrict(fric)
    return terms_list


def shards(
    temp, uvel, vvel, couple_col, couple_cell, cavity, thickness, viscosity, friction, drive
):
    ocean_rows = temp.shape[1]
    ocean_cols = temp.shape[2]
    whole_thick = lax.all_gather(thickness, "blk", axis=0, tiled=True)
    columns = couple_col.reshape(-1)
    cells = couple_cell.reshape(-1)
    top_entry = temp[0].reshape(-1)[columns]
    draft = whole_thick.reshape(-1)[cells]
    melt = cavity.reshape(-1).astype(jnp.float32) * melt_rate * (top_entry + 0.5 + 0.5 * draft)
    column_melt = jax.ops.segment_sum(melt, columns, ocean_rows * ocean_cols).reshape(
        ocean_rows, ocean_cols
    )
    padded = with_halo(jnp.stack([temp, uvel, vvel]), (("grp", 2), ("blk", 3)), 1)
    stepped = ocean_tendency(padded[0], padded[1], padded[2])
    temp_new = jnp.concatenate([stepped[:1] - melt_rate * column_melt[None], stepped[1:]], axis=0)
    dense = jax.ops.segment_sum(melt, cells, whole_thick.size).reshape(whole_thick.shape)
    owned = lax.psum_scatter(dense, "blk", scatter_dimension=0, tiled=True)
    melt_ice = lax.psum(owned, "grp")
    source = drive + melt_ice
    terms_list = level_terms(viscosity, friction, coeffs_halo)

    def operate_local(field, terms):
        return apply_padded(jnp.pad(cells_halo(field), ((0, 0), (1, 1))), terms)

    field = jnp.zeros_like(source)
    for cycle_index in range(CYCLES):
        field = vcycle(0, field, source, terms_list, operate_local)
    return (temp_new, field)


def solution(mesh):
    return jax.shard_map(
        shards,
        mesh=mesh,
        in_specs=(
            P(None, "grp", "blk"),
            P(None, "grp", "blk"),
            P(None, "grp", "blk"),
            P("grp", "blk", None),
            P("grp", "blk", None),
            P("grp", "blk", None),
            P("blk", None),
            P("blk", None),
            P("blk", None),
            P("blk", None),
        ),
        out_specs=(P(None, "grp", "blk"), P("blk", None)),
        check_vma=False,
    )
```

profile of v0, /device:TPU:12, one launch (start us, length us, event | category | flops | bytes accessed | tf_op | source)
XLA Modules:
  0.0 525.8 jit_solution(13978945496446045842)
XLA Ops:
  9.4 11.8 %gather_fusion = f32[2048]{0:T(1024)S(1)} fusion(f32[8192]{0:T(1024)S(1)} %slice_bitcast_fusion.3, s32[2048]{0:T(1024)S(1)} %broadcast_clamp_fusion.1), kind=kCustom, calls=%fused_computation | custom fusion | bytes 24576 | tf_op jit(solution)/shard_map/gather | solution.py:154
  21.3 25.0 %all-gather.2.cloned.1.call-done = f32[512,1024]{1,0:T(8,128)} async-done(((f32[128,1024]{1,0:T(8,128)}), f32[512,1024]{1,0:T(8,128)}) %all-gather.2.cloned.1.call-update) | async-done | bytes 2097168 | tf_op jit(solution)/shard_map/all_gather | solution.py:151
  48.4 11.8 %gather_fusion.1 = f32[2048]{0:T(1024)S(1)} fusion(f32[524288]{0:T(1024)S(1)} %bitcast.24, s32[2048]{0:T(1024)S(1)} %broadcast_clamp_fusion), kind=kCustom, calls=%fused_computation.1 | custom fusion | bytes 24576 | tf_op jit(solution)/shard_map/gather | solution.py:155
  60.2 11.8 %scatter_custom_fusion.1 = f32[524288]{0:T(1024)S(1)} fusion(s32[2048]{0:T(1024)S(1)} %bitcast.38, f32[2048]{0:T(1024)S(1)} %add_multiply_fusion.7, f32[]{:T(128)} %constant.35.clone.1), kind=kCustom, calls=%fused_computation.10 | custom fusion | flops 2048 | bytes 2097156 | tf_op jit(solution)/shard_map/scatter-add | solution.py:163
  73.5 3.5 collective-permute-start.6
  79.5 4.3 collective-permute-start.4
  85.8 5.3 %collective-permute-start.14 = (f32[1,512]{1,0:T(1,128)S(1)}, f32[1,512]{1,0:T(1,128)S(1)}, u32[]{:S(2)}, u32[]{:S(2)}) collective-permute-start(f32[1,512]{1,0:T(1,128)S(1)} %broadcast.253), channel_id=1, source_target_pairs={{1,0},{2,1},{3,2},{5,4},{6,5},{7,6},{9,8},{10,9},{11,10},{13,12},{... | collective-permute-start | bytes 6152 | tf_op jit(solution)/shard_map/ppermute | solution.py:26
  91.4 4.5 slice.914
  95.9 4.5 slice.915
  103.8 5.1 slice.924
  108.9 5.1 slice.925
  115.9 4.8 collective-permute-start.12
  123.6 4.8 collective-permute-start.22
  129.5 39.9 %all-reduce.39.cloned.1.call-done = f32[128,1024]{1,0:T(8,128)} async-done(((f32[128,1024]{1,0:T(8,128)}), f32[128,1024]{1,0:T(8,128)}) %all-reduce.39.cloned.1.call-update) | async-done | bytes 524304 | tf_op jit(solution)/shard_map/psum | solution.py:165
  171.7 3.4 collective-permute-start.8
  181.5 3.6 collective-permute-start.20
  186.1 3.9 collective-permute-start.10
  203.7 6.0 %slice.910 = f32[64,512]{1,0:T(8,128)} slice(f32[64,1024]{1,0:T(8,128)} %add.394), slice={[0:64:1], [0:1024:2]} | slice | bytes 262144 | tf_op jit(solution)/shard_map/slice | solution.py:55
  209.7 5.9 %slice.911 = f32[64,512]{1,0:T(8,128)} slice(f32[64,1024]{1,0:T(8,128)} %add.394), slice={[0:64:1], [1:1024:2]} | slice | bytes 262144 | tf_op jit(solution)/shard_map/slice | solution.py:55
  217.3 3.9 collective-permute-start.16
  224.6 3.0 collective-permute-done.17
  229.2 3.6 collective-permute-start.18
  259.4 3.9 collective-permute-start.24
  265.3 4.4 collective-permute-done.25
  272.7 3.9 collective-permute-start.27
  282.0 3.9 collective-permute-start.29
  295.1 3.9 collective-permute-start.31
  304.6 3.9 collective-permute-start.33
  318.5 4.1 collective-permute-start.35
  327.7 3.9 collective-permute-start.37
  337.0 3.9 collective-permute-start.39
  346.2 3.9 collective-permute-start.41
  355.5 3.9 collective-permute-start.43
  361.4 3.6 collective-permute-start.1
  372.0 5.9 %slice.1028 = f32[64,512]{1,0:T(8,128)} slice(f32[64,1024]{1,0:T(8,128)} %add.434), slice={[0:64:1], [0:1024:2]} | slice | bytes 262144 | tf_op jit(solution)/shard_map/slice | solution.py:55
  377.9 5.9 %slice.1029 = f32[64,512]{1,0:T(8,128)} slice(f32[64,1024]{1,0:T(8,128)} %add.434), slice={[0:64:1], [1:1024:2]} | slice | bytes 262144 | tf_op jit(solution)/shard_map/slice | solution.py:55
  387.8 3.0 collective-permute-start.45
  396.5 3.9 collective-permute-start.47
  408.0 4.8 collective-permute-start.3
  428.7 4.1 collective-permute-start.49
  438.8 2.9 collective-permute-start.50
  441.6 3.0 collective-permute-start.51
  451.7 3.0 collective-permute-start.53
  464.6 3.9 collective-permute-start.55
  474.2 3.9 collective-permute-start.57
  479.7 11.4 %scatter_custom_fusion = f32[8192]{0:T(1024)S(1)} fusion(s32[2048]{0:T(1024)} %bitcast.39, f32[2048]{0:T(1024)} %copy-done.43, f32[]{:T(128)} %constant.35.clone.1), kind=kCustom, calls=%fused_computation.508 | custom fusion | flops 2048 | bytes 33280 | tf_op jit(solution)/shard_map/scatter-add | solution.py:157
  501.6 3.0 collective-permute-start.59
  510.9 3.9 collective-permute-start.61
  (354 shorter events, 224.3 us)
Async XLA Ops:
  7.2 39.1 %all-gather.2.cloned.1.call-start = ((), (), s32[]{:S(2)}) async-start(), calls=%async_computation.1 | async-start | bytes 2621440 | tf_op jit(solution)/shard_map/all_gather | solution.py:151
  7.9 106.1 %reduce-scatter.2.cloned.1.call-start = ((), (), s32[]{:S(2)}) async-start(), calls=%async_computation.2 | async-start | bytes 2621440 | tf_op jit(solution)/shard_map/reduce_scatter | solution.py:164
  73.5 95.9 %all-reduce.39.cloned.1.call-start = ((), (), s32[]{:S(2)}) async-start(), calls=%async_computation.3 | async-start | bytes 1048576 | tf_op jit(solution)/shard_map/psum | solution.py:165
  73.5 47.5 %collective-permute-start.6 = (f32[1,1024]{1,0:T(1,128)S(1)}, f32[1,1024]{1,0:T(1,128)S(1)}, u32[]{:S(2)}, u32[]{:S(2)}) collective-permute-start(f32[1,1024]{1,0:T(1,128)S(1)} %broadcast.250), channel_id=1, source_target_pairs={{1,0},{2,1},{3,2},{5,4},{6,5},{7,6},{9,8},{10,9},{11,10},{13,12},{... | collective-permute-start | bytes 12296 | tf_op jit(solution)/shard_map/ppermute | solution.py:26
  77.1 45.9 %collective-permute-start.7 = (f32[1,1024]{1,0:T(1,128)S(1)}, f32[1,1024]{1,0:T(1,128)S(1)}, u32[]{:S(2)}, u32[]{:S(2)}) collective-permute-start(f32[1,1024]{1,0:T(1,128)S(1)} %broadcast.250), channel_id=1, source_target_pairs={{0,1},{1,2},{2,3},{4,5},{5,6},{6,7},{8,9},{9,10},{10,11},{12,13},{... | collective-permute-start | bytes 12296 | tf_op jit(solution)/shard_map/ppermute | solution.py:23
  79.5 34.4 %collective-permute-start.4 = (f32[1,1024]{1,0:T(1,128)S(1)}, f32[1,1024]{1,0:T(1,128)S(1)}, u32[]{:S(2)}, u32[]{:S(2)}) collective-permute-start(f32[1,1024]{1,0:T(1,128)S(1)} %get-tuple-element.49), channel_id=1, source_target_pairs={{1,0},{2,1},{3,2},{5,4},{6,5},{7,6},{9,8},{10,9},{11,10},{13,12},{... | collective-permute-start | bytes 12296 | tf_op jit(solution)/shard_map/ppermute | solution.py:26
  83.8 32.1 %collective-permute-start.5 = (f32[1,1024]{1,0:T(1,128)S(1)}, f32[1,1024]{1,0:T(1,128)S(1)}, u32[]{:S(2)}, u32[]{:S(2)}) collective-permute-start(f32[1,1024]{1,0:T(1,128)S(1)} %get-tuple-element.48), channel_id=1, source_target_pairs={{0,1},{1,2},{2,3},{4,5},{5,6},{6,7},{8,9},{9,10},{10,11},{12,13},{... | collective-permute-start | bytes 12296 | tf_op jit(solution)/shard_map/ppermute | solution.py:23
  85.8 100.3 %collective-permute-start.14 = (f32[1,512]{1,0:T(1,128)S(1)}, f32[1,512]{1,0:T(1,128)S(1)}, u32[]{:S(2)}, u32[]{:S(2)}) collective-permute-start(f32[1,512]{1,0:T(1,128)S(1)} %broadcast.253), channel_id=1, source_target_pairs={{1,0},{2,1},{3,2},{5,4},{6,5},{7,6},{9,8},{10,9},{11,10},{13,12},{... | collective-permute-start | bytes 6152 | tf_op jit(solution)/shard_map/ppermute | solution.py:26
  114.0 76.0 %collective-permute-start.15 = (f32[1,512]{1,0:T(1,128)S(1)}, f32[1,512]{1,0:T(1,128)S(1)}, u32[]{:S(2)}, u32[]{:S(2)}) collective-permute-start(f32[1,512]{1,0:T(1,128)S(1)} %broadcast.253), channel_id=1, source_target_pairs={{0,1},{1,2},{2,3},{4,5},{5,6},{6,7},{8,9},{9,10},{10,11},{12,13},{... | collective-permute-start | bytes 6152 | tf_op jit(solution)/shard_map/ppermute | solution.py:23
  115.9 55.8 %collective-permute-start.12 = (f32[1,512]{1,0:T(1,128)S(1)}, f32[1,512]{1,0:T(1,128)S(1)}, u32[]{:S(2)}, u32[]{:S(2)}) collective-permute-start(f32[1,512]{1,0:T(1,128)S(1)} %get-tuple-element.67), channel_id=1, source_target_pairs={{1,0},{2,1},{3,2},{5,4},{6,5},{7,6},{9,8},{10,9},{11,10},{13,12},{... | collective-permute-start | bytes 6152 | tf_op jit(solution)/shard_map/ppermute | solution.py:26
  121.0 54.1 %collective-permute-start.13 = (f32[1,512]{1,0:T(1,128)S(1)}, f32[1,512]{1,0:T(1,128)S(1)}, u32[]{:S(2)}, u32[]{:S(2)}) collective-permute-start(f32[1,512]{1,0:T(1,128)S(1)} %get-tuple-element.66), channel_id=1, source_target_pairs={{0,1},{1,2},{2,3},{4,5},{5,6},{6,7},{8,9},{9,10},{10,11},{12,13},{... | collective-permute-start | bytes 6152 | tf_op jit(solution)/shard_map/ppermute | solution.py:23
  123.6 112.0 %collective-permute-start.22 = (f32[1,256]{1,0:T(1,128)}, f32[1,256]{1,0:T(1,128)}, u32[]{:S(2)}, u32[]{:S(2)}) collective-permute-start(f32[1,256]{1,0:T(1,128)} %broadcast.256), channel_id=1, source_target_pairs={{1,0},{2,1},{3,2},{5,4},{6,5},{7,6},{9,8},{10,9},{11,10},{13,12},{... | collective-permute-start | bytes 3080 | tf_op jit(solution)/shard_map/ppermute | solution.py:26
  171.7 6.7 %collective-permute-start.8 = (f32[1,1024]{1,0:T(1,128)S(1)}, f32[1,1024]{1,0:T(1,128)S(1)}, u32[]{:S(2)}, u32[]{:S(2)}) collective-permute-start(f32[1,1024]{1,0:T(1,128)S(1)} %get-tuple-element.47), channel_id=1, source_target_pairs={{1,0},{2,1},{3,2},{5,4},{6,5},{7,6},{9,8},{10,9},{11,10},{13,12},{... | collective-permute-start | bytes 12296 | tf_op jit(solution)/shard_map/ppermute | solution.py:26
  175.1 6.4 %collective-permute-start.9 = (f32[1,1024]{1,0:T(1,128)S(1)}, f32[1,1024]{1,0:T(1,128)S(1)}, u32[]{:S(2)}, u32[]{:S(2)}) collective-permute-start(f32[1,1024]{1,0:T(1,128)S(1)} %get-tuple-element.46), channel_id=1, source_target_pairs={{0,1},{1,2},{2,3},{4,5},{5,6},{6,7},{8,9},{9,10},{10,11},{12,13},{... | collective-permute-start | bytes 12296 | tf_op jit(solution)/shard_map/ppermute | solution.py:23
  178.4 57.2 %collective-permute-start.23 = (f32[1,256]{1,0:T(1,128)}, f32[1,256]{1,0:T(1,128)}, u32[]{:S(2)}, u32[]{:S(2)}) collective-permute-start(f32[1,256]{1,0:T(1,128)} %broadcast.256), channel_id=1, source_target_pairs={{0,1},{1,2},{2,3},{4,5},{5,6},{6,7},{8,9},{9,10},{10,11},{12,13},{... | collective-permute-start | bytes 3080 | tf_op jit(solution)/shard_map/ppermute | solution.py:23
  181.5 39.7 %collective-permute-start.20 = (f32[1,256]{1,0:T(1,128)}, f32[1,256]{1,0:T(1,128)}, u32[]{:S(2)}, u32[]{:S(2)}) collective-permute-start(f32[1,256]{1,0:T(1,128)} %get-tuple-element.80), channel_id=1, source_target_pairs={{1,0},{2,1},{3,2},{5,4},{6,5},{7,6},{9,8},{10,9},{11,10},{13,12},{... | collective-permute-start | bytes 3080 | tf_op jit(solution)/shard_map/ppermute | solution.py:26
  186.1 7.9 %collective-permute-start.10 = (f32[1,1024]{1,0:T(1,128)S(1)}, f32[1,1024]{1,0:T(1,128)S(1)}, u32[]{:S(2)}, u32[]{:S(2)}) collective-permute-start(f32[1,1024]{1,0:T(1,128)S(1)} %get-tuple-element.45), channel_id=1, source_target_pairs={{1,0},{2,1},{3,2},{5,4},{6,5},{7,6},{9,8},{10,9},{11,10},{13,12},{... | collective-permute-start | bytes 12296 | tf_op jit(solution)/shard_map/ppermute | solution.py:26
  190.6 6.4 %collective-permute-start.11 = (f32[1,1024]{1,0:T(1,128)S(1)}, f32[1,1024]{1,0:T(1,128)S(1)}, u32[]{:S(2)}, u32[]{:S(2)}) collective-permute-start(f32[1,1024]{1,0:T(1,128)S(1)} %get-tuple-element.44), channel_id=1, source_target_pairs={{0,1},{1,2},{2,3},{4,5},{5,6},{6,7},{8,9},{9,10},{10,11},{12,13},{... | collective-permute-start | bytes 12296 | tf_op jit(solution)/shard_map/ppermute | solution.py:23
  194.0 29.2 %collective-permute-start.21 = (f32[1,256]{1,0:T(1,128)}, f32[1,256]{1,0:T(1,128)}, u32[]{:S(2)}, u32[]{:S(2)}) collective-permute-start(f32[1,256]{1,0:T(1,128)} %get-tuple-element.81), channel_id=1, source_target_pairs={{0,1},{1,2},{2,3},{4,5},{5,6},{6,7},{8,9},{9,10},{10,11},{12,13},{... | collective-permute-start | bytes 3080 | tf_op jit(solution)/shard_map/ppermute | solution.py:23
  217.3 7.4 %collective-permute-start.16 = (f32[1,512]{1,0:T(1,128)S(1)}, f32[1,512]{1,0:T(1,128)S(1)}, u32[]{:S(2)}, u32[]{:S(2)}) collective-permute-start(f32[1,512]{1,0:T(1,128)S(1)} %get-tuple-element.65), channel_id=1, source_target_pairs={{1,0},{2,1},{3,2},{5,4},{6,5},{7,6},{9,8},{10,9},{11,10},{13,12},{... | collective-permute-start | bytes 6152 | tf_op jit(solution)/shard_map/ppermute | solution.py:26
  221.2 6.4 %collective-permute-start.17 = (f32[1,512]{1,0:T(1,128)S(1)}, f32[1,512]{1,0:T(1,128)S(1)}, u32[]{:S(2)}, u32[]{:S(2)}) collective-permute-start(f32[1,512]{1,0:T(1,128)S(1)} %get-tuple-element.64), channel_id=1, source_target_pairs={{0,1},{1,2},{2,3},{4,5},{5,6},{6,7},{8,9},{9,10},{10,11},{12,13},{... | collective-permute-start | bytes 6152 | tf_op jit(solution)/shard_map/ppermute | solution.py:23
  229.2 15.7 %collective-permute-start.18 = (f32[1,512]{1,0:T(1,128)}, f32[1,512]{1,0:T(1,128)}, u32[]{:S(2)}, u32[]{:S(2)}) collective-permute-start(f32[1,512]{1,0:T(1,128)} %get-tuple-element.63), channel_id=1, source_target_pairs={{1,0},{2,1},{3,2},{5,4},{6,5},{7,6},{9,8},{10,9},{11,10},{13,12},{... | collective-permute-start | bytes 6152 | tf_op jit(solution)/shard_map/ppermute | solution.py:26
  232.7 12.2 %collective-permute-start.19 = (f32[1,512]{1,0:T(1,128)}, f32[1,512]{1,0:T(1,128)}, u32[]{:S(2)}, u32[]{:S(2)}) collective-permute-start(f32[1,512]{1,0:T(1,128)} %get-tuple-element.62), channel_id=1, source_target_pairs={{0,1},{1,2},{2,3},{4,5},{5,6},{6,7},{8,9},{9,10},{10,11},{12,13},{... | collective-permute-start | bytes 6152 | tf_op jit(solution)/shard_map/ppermute | solution.py:23
  295.1 6.4 %collective-permute-start.31 = (f32[1,512]{1,0:T(1,128)S(1)}, f32[1,512]{1,0:T(1,128)S(1)}, u32[]{:S(2)}, u32[]{:S(2)}) collective-permute-start(f32[1,512]{1,0:T(1,128)S(1)} %get-tuple-element.60), channel_id=1, source_target_pairs={{0,1},{1,2},{2,3},{4,5},{5,6},{6,7},{8,9},{9,10},{10,11},{12,13},{... | collective-permute-start | bytes 6152 | tf_op jit(solution)/shard_map/ppermute | solution.py:23
  304.6 6.4 %collective-permute-start.33 = (f32[1,512]{1,0:T(1,128)S(1)}, f32[1,512]{1,0:T(1,128)S(1)}, u32[]{:S(2)}, u32[]{:S(2)}) collective-permute-start(f32[1,512]{1,0:T(1,128)S(1)} %get-tuple-element.58), channel_id=1, source_target_pairs={{0,1},{1,2},{2,3},{4,5},{5,6},{6,7},{8,9},{9,10},{10,11},{12,13},{... | collective-permute-start | bytes 6152 | tf_op jit(solution)/shard_map/ppermute | solution.py:23
  318.5 6.4 %collective-permute-start.35 = (f32[1,1024]{1,0:T(1,128)S(1)}, f32[1,1024]{1,0:T(1,128)S(1)}, u32[]{:S(2)}, u32[]{:S(2)}) collective-permute-start(f32[1,1024]{1,0:T(1,128)S(1)} %get-tuple-element.42), channel_id=1, source_target_pairs={{0,1},{1,2},{2,3},{4,5},{5,6},{6,7},{8,9},{9,10},{10,11},{12,13},{... | collective-permute-start | bytes 12296 | tf_op jit(solution)/shard_map/ppermute | solution.py:23
  327.7 6.4 %collective-permute-start.37 = (f32[1,1024]{1,0:T(1,128)S(1)}, f32[1,1024]{1,0:T(1,128)S(1)}, u32[]{:S(2)}, u32[]{:S(2)}) collective-permute-start(f32[1,1024]{1,0:T(1,128)S(1)} %get-tuple-element.40), channel_id=1, source_target_pairs={{0,1},{1,2},{2,3},{4,5},{5,6},{6,7},{8,9},{9,10},{10,11},{12,13},{... | collective-permute-start | bytes 12296 | tf_op jit(solution)/shard_map/ppermute | solution.py:23
  337.0 6.4 %collective-permute-start.39 = (f32[1,1024]{1,0:T(1,128)S(1)}, f32[1,1024]{1,0:T(1,128)S(1)}, u32[]{:S(2)}, u32[]{:S(2)}) collective-permute-start(f32[1,1024]{1,0:T(1,128)S(1)} %get-tuple-element.38), channel_id=1, source_target_pairs={{0,1},{1,2},{2,3},{4,5},{5,6},{6,7},{8,9},{9,10},{10,11},{12,13},{... | collective-permute-start | bytes 12296 | tf_op jit(solution)/shard_map/ppermute | solution.py:23
  346.2 6.4 %collective-permute-start.41 = (f32[1,1024]{1,0:T(1,128)S(1)}, f32[1,1024]{1,0:T(1,128)S(1)}, u32[]{:S(2)}, u32[]{:S(2)}) collective-permute-start(f32[1,1024]{1,0:T(1,128)S(1)} %get-tuple-element.36), channel_id=1, source_target_pairs={{0,1},{1,2},{2,3},{4,5},{5,6},{6,7},{8,9},{9,10},{10,11},{12,13},{... | collective-permute-start | bytes 12296 | tf_op jit(solution)/shard_map/ppermute | solution.py:23
  353.6 11.5 %collective-permute-start.42 = (f32[1,1024]{1,0:T(1,128)S(1)}, f32[1,1024]{1,0:T(1,128)S(1)}, u32[]{:S(2)}, u32[]{:S(2)}) collective-permute-start(f32[1,1024]{1,0:T(1,128)S(1)} %get-tuple-element.35), channel_id=1, source_target_pairs={{1,0},{2,1},{3,2},{5,4},{6,5},{7,6},{9,8},{10,9},{11,10},{13,12},{... | collective-permute-start | bytes 12296 | tf_op jit(solution)/shard_map/ppermute | solution.py:26
  355.5 9.6 %collective-permute-start.43 = (f32[1,1024]{1,0:T(1,128)S(1)}, f32[1,1024]{1,0:T(1,128)S(1)}, u32[]{:S(2)}, u32[]{:S(2)}) collective-permute-start(f32[1,1024]{1,0:T(1,128)S(1)} %get-tuple-element.34), channel_id=1, source_target_pairs={{0,1},{1,2},{2,3},{4,5},{5,6},{6,7},{8,9},{9,10},{10,11},{12,13},{... | collective-permute-start | bytes 12296 | tf_op jit(solution)/shard_map/ppermute | solution.py:23
  359.5 31.4 %collective-permute-start = (f32[3,8,1,128]{3,2,1,0:T(1,128)S(1)}, f32[3,8,1,128]{3,2,1,0:T(1,128)S(1)}, u32[]{:S(2)}, u32[]{:S(2)}) collective-permute-start(f32[3,8,1,128]{3,2,1,0:T(1,128)S(1)} %get-tuple-element.28), channel_id=1, source_target_pairs={{0,4},{4,8},{8,12},{12,16},{16,20},{20,24},{24,28},{1,5},{5,9},{9,... | collective-permute-start | bytes 36872 | tf_op jit(solution)/shard_map/ppermute | solution.py:23
  361.4 29.5 %collective-permute-start.1 = (f32[3,8,1,128]{3,2,1,0:T(1,128)S(1)}, f32[3,8,1,128]{3,2,1,0:T(1,128)S(1)}, u32[]{:S(2)}, u32[]{:S(2)}) collective-permute-start(f32[3,8,1,128]{3,2,1,0:T(1,128)S(1)} %get-tuple-element.29), channel_id=1, source_target_pairs={{4,0},{8,4},{12,8},{16,12},{20,16},{24,20},{28,24},{5,1},{9,5},{13... | collective-permute-start | bytes 36872 | tf_op jit(solution)/shard_map/ppermute | solution.py:26
  385.0 7.1 %collective-permute-start.44 = (f32[1,512]{1,0:T(1,128)S(1)}, f32[1,512]{1,0:T(1,128)S(1)}, u32[]{:S(2)}, u32[]{:S(2)}) collective-permute-start(f32[1,512]{1,0:T(1,128)S(1)} %get-tuple-element.57), channel_id=1, source_target_pairs={{1,0},{2,1},{3,2},{5,4},{6,5},{7,6},{9,8},{10,9},{11,10},{13,12},{... | collective-permute-start | bytes 6152 | tf_op jit(solution)/shard_map/ppermute | solution.py:26
  394.5 18.3 %collective-permute-start.46 = (f32[1,512]{1,0:T(1,128)S(1)}, f32[1,512]{1,0:T(1,128)S(1)}, u32[]{:S(2)}, u32[]{:S(2)}) collective-permute-start(f32[1,512]{1,0:T(1,128)S(1)} %get-tuple-element.55), channel_id=1, source_target_pairs={{1,0},{2,1},{3,2},{5,4},{6,5},{7,6},{9,8},{10,9},{11,10},{13,12},{... | collective-permute-start | bytes 6152 | tf_op jit(solution)/shard_map/ppermute | solution.py:26
  396.5 16.4 %collective-permute-start.47 = (f32[1,512]{1,0:T(1,128)S(1)}, f32[1,512]{1,0:T(1,128)S(1)}, u32[]{:S(2)}, u32[]{:S(2)}) collective-permute-start(f32[1,512]{1,0:T(1,128)S(1)} %get-tuple-element.54), channel_id=1, source_target_pairs={{0,1},{1,2},{2,3},{4,5},{5,6},{6,7},{8,9},{9,10},{10,11},{12,13},{... | collective-permute-start | bytes 6152 | tf_op jit(solution)/shard_map/ppermute | solution.py:23
  404.0 28.9 %collective-permute-start.2 = (f32[3,8,66,1]{2,1,3,0:T(8,128)}, f32[3,8,66,1]{2,1,3,0:T(8,128)}, u32[]{:S(2)}, u32[]{:S(2)}) collective-permute-start(f32[3,8,66,1]{2,1,3,0:T(8,128)} %copy.16), channel_id=1, source_target_pairs={{0,1},{1,2},{2,3},{4,5},{5,6},{6,7},{8,9},{9,10},{10,11},{12,13},{... | collective-permute-start | bytes 19016 | tf_op jit(solution)/shard_map/ppermute | solution.py:23
  408.0 26.8 %collective-permute-start.3 = (f32[3,8,66,1]{2,1,3,0:T(8,128)}, f32[3,8,66,1]{2,1,3,0:T(8,128)}, u32[]{:S(2)}, u32[]{:S(2)}) collective-permute-start(f32[3,8,66,1]{2,1,3,0:T(8,128)} %copy.17), channel_id=1, source_target_pairs={{1,0},{2,1},{3,2},{5,4},{6,5},{7,6},{9,8},{10,9},{11,10},{13,12},{... | collective-permute-start | bytes 19016 | tf_op jit(solution)/shard_map/ppermute | solution.py:26
  426.2 10.7 %collective-permute-start.48 = (f32[1,256]{1,0:T(1,128)}, f32[1,256]{1,0:T(1,128)}, u32[]{:S(2)}, u32[]{:S(2)}) collective-permute-start(f32[1,256]{1,0:T(1,128)} %get-tuple-element.73), channel_id=1, source_target_pairs={{1,0},{2,1},{3,2},{5,4},{6,5},{7,6},{9,8},{10,9},{11,10},{13,12},{... | collective-permute-start | bytes 3080 | tf_op jit(solution)/shard_map/ppermute | solution.py:26
  428.7 8.2 %collective-permute-start.49 = (f32[1,256]{1,0:T(1,128)}, f32[1,256]{1,0:T(1,128)}, u32[]{:S(2)}, u32[]{:S(2)}) collective-permute-start(f32[1,256]{1,0:T(1,128)} %get-tuple-element.72), channel_id=1, source_target_pairs={{0,1},{1,2},{2,3},{4,5},{5,6},{6,7},{8,9},{9,10},{10,11},{12,13},{... | collective-permute-start | bytes 3080 | tf_op jit(solution)/shard_map/ppermute | solution.py:23
  438.8 8.3 %collective-permute-start.50 = (f32[1,256]{1,0:T(1,128)S(1)}, f32[1,256]{1,0:T(1,128)S(1)}, u32[]{:S(2)}, u32[]{:S(2)}) collective-permute-start(f32[1,256]{1,0:T(1,128)S(1)} %get-tuple-element.71), channel_id=1, source_target_pairs={{1,0},{2,1},{3,2},{5,4},{6,5},{7,6},{9,8},{10,9},{11,10},{13,12},{... | collective-permute-start | bytes 3080 | tf_op jit(solution)/shard_map/ppermute | solution.py:26
  448.9 7.0 %collective-permute-start.52 = (f32[1,256]{1,0:T(1,128)S(1)}, f32[1,256]{1,0:T(1,128)S(1)}, u32[]{:S(2)}, u32[]{:S(2)}) collective-permute-start(f32[1,256]{1,0:T(1,128)S(1)} %get-tuple-element.69), channel_id=1, source_target_pairs={{1,0},{2,1},{3,2},{5,4},{6,5},{7,6},{9,8},{10,9},{11,10},{13,12},{... | collective-permute-start | bytes 3080 | tf_op jit(solution)/shard_map/ppermute | solution.py:26
  472.3 18.8 %collective-permute-start.56 = (f32[1,512]{1,0:T(1,128)S(1)}, f32[1,512]{1,0:T(1,128)S(1)}, u32[]{:S(2)}, u32[]{:S(2)}) collective-permute-start(f32[1,512]{1,0:T(1,128)S(1)} %get-tuple-element.51), channel_id=1, source_target_pairs={{1,0},{2,1},{3,2},{5,4},{6,5},{7,6},{9,8},{10,9},{11,10},{13,12},{... | collective-permute-start | bytes 6152 | tf_op jit(solution)/shard_map/ppermute | solution.py:26
  474.2 16.9 %collective-permute-start.57 = (f32[1,512]{1,0:T(1,128)S(1)}, f32[1,512]{1,0:T(1,128)S(1)}, u32[]{:S(2)}, u32[]{:S(2)}) collective-permute-start(f32[1,512]{1,0:T(1,128)S(1)} %get-tuple-element.50), channel_id=1, source_target_pairs={{0,1},{1,2},{2,3},{4,5},{5,6},{6,7},{8,9},{9,10},{10,11},{12,13},{... | collective-permute-start | bytes 6152 | tf_op jit(solution)/shard_map/ppermute | solution.py:23
  498.8 6.6 %collective-permute-start.58 = (f32[1,1024]{1,0:T(1,128)S(1)}, f32[1,1024]{1,0:T(1,128)S(1)}, u32[]{:S(2)}, u32[]{:S(2)}) collective-permute-start(f32[1,1024]{1,0:T(1,128)S(1)} %get-tuple-element.33), channel_id=1, source_target_pairs={{1,0},{2,1},{3,2},{5,4},{6,5},{7,6},{9,8},{10,9},{11,10},{13,12},{... | collective-permute-start | bytes 12296 | tf_op jit(solution)/shard_map/ppermute | solution.py:26
  501.6 6.4 %collective-permute-start.59 = (f32[1,1024]{1,0:T(1,128)S(1)}, f32[1,1024]{1,0:T(1,128)S(1)}, u32[]{:S(2)}, u32[]{:S(2)}) collective-permute-start(f32[1,1024]{1,0:T(1,128)S(1)} %get-tuple-element.32), channel_id=1, source_target_pairs={{0,1},{1,2},{2,3},{4,5},{5,6},{6,7},{8,9},{9,10},{10,11},{12,13},{... | collective-permute-start | bytes 12296 | tf_op jit(solution)/shard_map/ppermute | solution.py:23
  509.0 6.6 %collective-permute-start.60 = (f32[1,1024]{1,0:T(1,128)S(1)}, f32[1,1024]{1,0:T(1,128)S(1)}, u32[]{:S(2)}, u32[]{:S(2)}) collective-permute-start(f32[1,1024]{1,0:T(1,128)S(1)} %get-tuple-element.31), channel_id=1, source_target_pairs={{1,0},{2,1},{3,2},{5,4},{6,5},{7,6},{9,8},{10,9},{11,10},{13,12},{... | collective-permute-start | bytes 12296 | tf_op jit(solution)/shard_map/ppermute | solution.py:26
  510.9 6.4 %collective-permute-start.61 = (f32[1,1024]{1,0:T(1,128)S(1)}, f32[1,1024]{1,0:T(1,128)S(1)}, u32[]{:S(2)}, u32[]{:S(2)}) collective-permute-start(f32[1,1024]{1,0:T(1,128)S(1)} %get-tuple-element.30), channel_id=1, source_target_pairs={{0,1},{1,2},{2,3},{4,5},{5,6},{6,7},{8,9},{9,10},{10,11},{12,13},{... | collective-permute-start | bytes 12296 | tf_op jit(solution)/shard_map/ppermute | solution.py:23
  (66 other events, 969.2 us)
Sparse Core Ops, SparseCore 0:
  9.8 36.4 all-gather.1
  73.6 35.3 reduce-scatter.1
  114.1 55.2 all-reduce.38
where the time goes:
time: 533 us; the launch traced here: 526 us
  starting transfers between devices  187 us (35%)
  local copies, waits for them, and re-layouts  131 us (25%)
  waiting for transfers between devices  106 us (20%)
  other arithmetic  80.5 us (15%)
  between operations  16 us (3%)
  matrix products  5.56 us (1%)
    ppermute x31, starting transfers between devices, with_halo(): lax.ppermute(lax.slice_in_dim(block, block.shape[dim] - width, None, axis...  94.4 us
    ppermute x31, starting transfers between devices, with_halo(): lax.ppermute(lax.slice_in_dim(block, 0, width, axis=dim), axis, backward)  92.3 us
    slice x16, local copies, waits for them, and re-layouts, restrict(): return 0.25 * (paired[:, 0::2] + paired[:, 1::2])  60.6 us
    ppermute x31, waiting for transfers between devices, with_halo(): lax.ppermute(lax.slice_in_dim(block, block.shape[dim] - width, None, axis...  40.7 us
    psum x1, waiting for transfers between devices, shards(): melt_ice = lax.psum(owned, 'grp')  39.9 us
    all_gather x1, waiting for transfers between devices, shards(): whole_thick = lax.all_gather(thickness, 'blk', axis=0, tiled=True)  25 us
    concatenate x31, other arithmetic, with_halo(): block = jnp.concatenate([low, block, high], axis=dim)  16.4 us
    slice x16, local copies, waits for them, and re-layouts, restrict(): paired = field[0::2] + field[1::2]  14.9 us
  transfers between devices with their start and end apart: 65, of which 20 were waited for; matrix products, arithmetic and copies ran while one was open for 26% of the time, Pallas kernels for 0%

commit v1 on v0

v1 whole, which is shorter than its diff:
```python
import functools

import jax
import jax.numpy as jnp
from jax import lax
from jax.experimental import pallas as pl
from jax.experimental.pallas import tpu as pltpu
from jax.sharding import PartitionSpec as P

LEVELS = 3
SMOOTH_SWEEPS = 2
COARSE_SWEEPS = 4
CYCLES = 2

omega = 0.8
kappa = 0.1
vertical_mix = 0.2
melt_rate = 0.5

MESH = pl.DeviceIdType.MESH
VM = pl.BlockSpec(memory_space=pltpu.VMEM)
LIMIT = 56 * 1024 * 1024
F32 = jnp.float32
BF16 = jnp.bfloat16


def split(x):
    high = x.astype(BF16).astype(F32)
    return high, x - high


def dot2(x, one, left=False):
    out = None
    for part in split(x):
        part = part.astype(BF16)
        term = jnp.dot(one, part, preferred_element_type=F32) if left else jnp.dot(
            part, one, preferred_element_type=F32)
        out = term if out is None else out + term
    return out


def nt(a, b):
    return lax.dot_general(a, b, (((1,), (1,)), ((), ())), preferred_element_type=F32)


def iota(shape, dim):
    return lax.broadcasted_iota(jnp.int32, shape, dim)


def remote(src, dst, send, recv, device):
    return pltpu.make_async_remote_copy(
        src_ref=src, dst_ref=dst, send_sem=send, recv_sem=recv, device_id=device,
        device_id_type=MESH)


def couple_kernel(n_grp, n_blk, temp0, col, cell, cav, thick, visc, fric, row_edge, col_edge,
                  part_out, draft_out, top_out, visc_out, fric_out, row_out, col_out,
                  ent_cell, ent_cav, ent_w, acc, dsem_s, dsem_r, hsem_s, hsem_r):
    g = lax.axis_index("grp")
    b = lax.axis_index("blk")
    core = lax.rem(g, 2)
    rows, cols = thick.shape
    count = cell.shape[1]
    half = rows // 2
    up_g, dn_g = lax.rem(g + 1, n_grp), lax.rem(g + n_grp - 1, n_grp)
    up_b, dn_b = lax.rem(b + 1, n_blk), lax.rem(b + n_blk - 1, n_blk)

    barrier = pltpu.get_barrier_semaphore()
    peers = [(g, lax.rem(b + k, n_blk)) for k in range(1, n_blk)]
    for device in peers + [(up_g, b), (dn_g, b)]:
        pl.semaphore_signal(barrier, inc=1, device_id=device, device_id_type=MESH)
    pl.semaphore_wait(barrier, n_blk + 1)

    ent = []
    for k in range(1, n_blk):
        target = peers[k - 1]
        trio = [
            remote(cell, ent_cell.at[k - 1], dsem_s.at[k - 1, 0], dsem_r.at[k - 1, 0], target),
            remote(cav, ent_cav.at[k - 1], dsem_s.at[k - 1, 1], dsem_r.at[k - 1, 1], target),
            remote(ent_w.at[0], ent_w.at[k], dsem_s.at[k - 1, 2], dsem_r.at[k - 1, 2], target),
        ]
        trio[0].start()
        trio[1].start()
        ent.append(trio)

    ids = col[...]
    ocean_rows, ocean_cols = temp0.shape
    row = ids // ocean_cols
    lane = ids - row * ocean_cols
    pick = (iota((ocean_cols, count), 0) == lane).astype(F32).astype(BF16)
    wide = dot2(temp0[...], pick)
    low = temp0[...] - split(temp0[...])[0]
    rest = split(low)[1]
    wide = wide + jnp.dot(rest.astype(BF16), pick, preferred_element_type=F32)
    top = jnp.sum(jnp.where(iota((ocean_rows, count), 0) == row, wide, 0.0), axis=0, keepdims=True)
    top_out[...] = top
    ent_w[0] = cav[...].astype(F32) * melt_rate * (top + 0.5)
    for trio in ent:
        trio[2].start()

    edges = [
        remote(row_edge.at[1], row_out.at[0], hsem_s.at[0], hsem_r.at[0], (up_g, b)),
        remote(row_edge.at[0], row_out.at[1], hsem_s.at[1], hsem_r.at[1], (dn_g, b)),
        remote(col_edge.at[1], col_out.at[0], hsem_s.at[2], hsem_r.at[2], (g, up_b)),
        remote(col_edge.at[0], col_out.at[1], hsem_s.at[3], hsem_r.at[3], (g, dn_b)),
    ]
    for copy in edges:
        copy.start()
    own = pl.multiple_of((1 - core) * half, 8)
    halo = pl.multiple_of(core * 2 * half, 8)
    target = (g, lax.rem(b + n_blk + 1 - 2 * core, n_blk))
    does = jnp.where(core == 0, b < n_blk - 1, b > 0)
    gets = jnp.where(core == 0, b > 0, b < n_blk - 1)
    ice = [
        remote(visc.at[pl.ds(own, half)], visc_out.at[pl.ds(halo, half)], hsem_s.at[4],
               hsem_r.at[4], target),
        remote(fric.at[pl.ds(own, half)], fric_out.at[pl.ds(halo, half)], hsem_s.at[5],
               hsem_r.at[5], target),
    ]

    @pl.when(does)
    def _():
        for copy in ice:
            copy.start()

    inside = pl.multiple_of((1 - core) * half, 8)
    visc_out[pl.ds(inside, 2 * half), :] = visc[...]
    fric_out[pl.ds(inside, 2 * half), :] = fric[...]

    @pl.when(jnp.logical_not(gets))
    def _():
        visc_out[pl.ds(halo, half), :] = jnp.zeros((half, cols), F32)
        fric_out[pl.ds(halo, half), :] = jnp.ones((half, cols), F32)

    high, low = split(thick[...])
    thick2 = jnp.concatenate([high, low], axis=0).astype(BF16)
    acc[...] = jnp.zeros_like(acc)
    chunk = 512
    for k in range(n_blk):
        if k > 0:
            for copy in ent[k - 1]:
                copy.wait_recv()
        cells_ref = cell if k == 0 else ent_cell.at[k - 1]
        cav_ref = cav if k == 0 else ent_cav.at[k - 1]

        for part in range(count // chunk):
            at = slice(part * chunk, (part + 1) * chunk)
            cells = cells_ref[:, at]
            grid_row = cells // cols
            lane = cells - grid_row * cols
            hit = iota((rows, chunk), 0) == grid_row - b * rows
            pick = (iota((cols, chunk), 0) == lane).astype(F32).astype(BF16)
            w_high, w_low = split(ent_w[k, :, at])
            spread = jnp.concatenate(
                [
                    jnp.where(hit, w_high, 0.0).astype(BF16),
                    jnp.where(hit, w_low, 0.0).astype(BF16),
                    jnp.where(hit, cav_ref[:, at].astype(F32), 0.0).astype(BF16),
                ], axis=0)
            acc[...] += nt(spread, pick)
            drafts = jnp.dot(thick2, pick, preferred_element_type=F32)
            draft_out[k, :, at] = jnp.sum(
                jnp.where(hit, drafts[:rows] + drafts[rows:], 0.0), axis=0, keepdims=True)

    part_out[...] = acc[:rows] + acc[rows:2 * rows] + (0.5 * melt_rate) * acc[2 * rows:] * thick[...]

    for trio in ent:
        for copy in trio:
            copy.wait_send()
    for copy in edges:
        copy.wait()

    @pl.when(does)
    def _():
        for copy in ice:
            copy.wait_send()

    @pl.when(gets)
    def _():
        for copy in ice:
            copy.wait_recv()


def reduce_kernel(n_grp, n_blk, part, drive, drafts, source, draft_out,
                  near, pair, far, dback, sem_s, sem_r, dsem_s, dsem_r):
    g = lax.axis_index("grp")
    b = lax.axis_index("blk")
    core = lax.rem(g, 2)
    rows, cols = part.shape
    half = rows // 2
    nz = n_grp // 2
    z = g // 2
    size = half // nz
    partner = g + 1 - 2 * core

    barrier = pltpu.get_barrier_semaphore()
    zpeers = [(lax.rem(g + 2 * k, n_grp), b) for k in range(1, nz)]
    bpeers = [(g, lax.rem(b + n_blk - k, n_blk)) for k in range(1, n_blk)]
    outer = (partner, lax.rem(b + n_blk - 1 + 2 * core, n_blk))
    out_does = jnp.where(core == 0, b > 0, b < n_blk - 1)
    for device in zpeers + bpeers + [(partner, b), outer]:
        pl.semaphore_signal(barrier, inc=1, device_id=device, device_id_type=MESH)
    pl.semaphore_wait(barrier, nz - 1 + n_blk - 1 + 2)

    give = pl.multiple_of((1 - core) * half, 8)
    keep = pl.multiple_of(core * half, 8)
    first = remote(part.at[pl.ds(give, half)], pair, sem_s.at[0], sem_r.at[0], (partner, b))
    first.start()
    back = [
        remote(drafts.at[k], dback.at[k - 1], dsem_s.at[k - 1], dsem_r.at[k - 1], bpeers[k - 1])
        for k in range(1, n_blk)
    ]
    for copy in back:
        copy.start()
    first.wait_recv()
    near[...] = part[pl.ds(keep, half), :] + pair[...]

    scatter = []
    for k in range(1, nz):
        to = lax.rem(z + k, nz)
        copy = remote(near.at[pl.ds(pl.multiple_of(to * size, 8), size)], far.at[k - 1],
                      sem_s.at[k], sem_r.at[k], zpeers[k - 1])
        copy.start()
        scatter.append(copy)
    mine = pl.multiple_of(z * size, 8)
    total = near[pl.ds(mine, size), :] + drive[pl.ds(pl.multiple_of(core * half + z * size, 8), size), :]
    for k in range(1, nz):
        scatter[k - 1].wait_recv()
        total = total + far[k - 1]
    source[pl.ds(pl.multiple_of(half + z * size, 8), size), :] = total

    spread = []
    for k in range(1, nz):
        block = source.at[pl.ds(pl.multiple_of(half + z * size, 8), size)]
        copy = remote(block, block, sem_s.at[nz + k], sem_r.at[nz + k], zpeers[k - 1])
        copy.start()
        spread.append(copy)
    for copy in spread:
        copy.wait_recv()

    middle = source.at[pl.ds(half, half)]
    there = pl.multiple_of(core * 2 * half, 8)
    away = pl.multiple_of((1 - core) * 2 * half, 8)
    swap = remote(middle, source.at[pl.ds(there, half)], sem_s.at[2 * nz], sem_r.at[2 * nz],
                  (partner, b))
    edge = remote(middle, source.at[pl.ds(away, half)], sem_s.at[2 * nz + 1],
                  sem_r.at[2 * nz + 1], outer)
    swap.start()

    @pl.when(out_does)
    def _():
        edge.start()

    @pl.when(jnp.logical_not(out_does))
    def _():
        source[pl.ds(there, half), :] = jnp.zeros((half, cols), F32)

    total = drafts[0]
    for k in range(1, n_blk):
        back[k - 1].wait_recv()
        total = total + dback[k - 1]
    draft_out[...] = total

    first.wait_send()
    for copy in back + scatter + spread:
        copy.wait_send()
    swap.wait()

    @pl.when(out_does)
    def _():
        edge.wait()


def swap_kernel(block, out, sem_s, sem_r):
    g = lax.axis_index("grp")
    b = lax.axis_index("blk")
    core = lax.rem(g, 2)
    partner = (g + 1 - 2 * core, b)
    half = block.shape[0]
    barrier = pltpu.get_barrier_semaphore()
    pl.semaphore_signal(barrier, inc=1, device_id=partner, device_id_type=MESH)
    pl.semaphore_wait(barrier, 1)
    here = pl.multiple_of(core * half, 8)
    copy = remote(block, out.at[pl.ds(here, half)], sem_s, sem_r, partner)
    copy.start()
    out[pl.ds(here, half), :] = block[...]
    copy.wait()


def ocean_kernel(n_grp, n_blk, temp, uvel, vvel, row_edge, col_edge, col, cav, top, draft, out):
    g = lax.axis_index("grp")
    b = lax.axis_index("blk")
    levels, rows, cols = temp.shape
    count = col.shape[1]
    melt = cav[...].astype(F32) * melt_rate * (top[...] + 0.5 + 0.5 * draft[...])
    ids = col[...]
    row = ids // cols
    lane = ids - row * cols
    hit = iota((rows, count), 0) == row
    pick = (iota((cols, count), 0) == lane).astype(F32).astype(BF16)
    high, low = split(melt)
    surface = nt(jnp.where(hit, high, 0.0).astype(BF16), pick)
    surface = surface + nt(jnp.where(hit, low, 0.0).astype(BF16), pick)

    west_in = (g > 0).astype(F32)
    east_in = (g < n_grp - 1).astype(F32)
    south_in = (b > 0).astype(F32)
    north_in = (b < n_blk - 1).astype(F32)
    at_row = iota((rows, cols), 0)
    at_col = iota((rows, cols), 1)

    def four(x, which, rowwise, colwise, k):
        found = []
        if rowwise:
            low = row_edge[0, which, k:k + 1, :] * west_in
            high = row_edge[1, which, k:k + 1, :] * east_in
            found.append(jnp.where(at_row == rows - 1, high, pltpu.roll(x, rows - 1, 0)))
            found.append(jnp.where(at_row == 0, low, pltpu.roll(x, 1, 0)))
        if colwise:
            low = col_edge[0, which, k] * south_in
            high = col_edge[1, which, k] * north_in
            found.append(jnp.where(at_col == cols - 1, high, pltpu.roll(x, cols - 1, 1)))
            found.append(jnp.where(at_col == 0, low, pltpu.roll(x, 1, 1)))
        return found

    for k in range(levels):
        t = temp[k]
        u = uvel[k]
        v = vvel[k]
        te, tw, tn, ts = four(t, 0, True, True, k)
        ue, uw = four(u, 1, True, False, k)
        vn, vs = four(v, 1, False, True, k)
        ue = 0.5 * (u + ue)
        uw = 0.5 * (u + uw)
        vn = 0.5 * (v + vn)
        vs = 0.5 * (v + vs)
        flux_east = jnp.maximum(ue, 0.0) * t + jnp.minimum(ue, 0.0) * te
        flux_west = jnp.maximum(uw, 0.0) * tw + jnp.minimum(uw, 0.0) * t
        flux_north = jnp.maximum(vn, 0.0) * t + jnp.minimum(vn, 0.0) * tn
        flux_south = jnp.maximum(vs, 0.0) * ts + jnp.minimum(vs, 0.0) * t
        laplace = te + tw + tn + ts - 4.0 * t
        vert = jnp.zeros_like(t)
        if k + 1 < levels:
            vert = vert + (temp[k + 1] - t)
        if k > 0:
            vert = vert - (t - temp[k - 1])
        new = (t + flux_west - flux_east + flux_south - flux_north + kappa * laplace
               + vertical_mix * vert)
        if k == 0:
            new = new - melt_rate * surface
        out[k] = new


def shift_rows(before, now, after):
    rows = now.shape[0]
    at = iota(now.shape, 0)
    above = jnp.where(at == 0, pltpu.roll(before, 1, 0), pltpu.roll(now, 1, 0))
    below = jnp.where(at == rows - 1, pltpu.roll(after, rows - 1, 0), pltpu.roll(now, rows - 1, 0))
    return above, below


def solve_kernel(n_blk, source, visc, fric, out, *scratch):
    g = lax.axis_index("grp")
    b = lax.axis_index("blk")
    core = lax.rem(g, 2)
    ext, wide = source.shape
    step = 8
    sizes = [(ext >> d, wide >> d) for d in range(LEVELS)]
    names = ("visc", "fric", "f", "a", "b", "e", "w", "n", "s", "d", "i")
    lev = [dict(zip(names, scratch[d * len(names):(d + 1) * len(names)])) for d in range(LEVELS)]
    down, right, up, left = scratch[LEVELS * len(names):]

    r, c = down.shape
    down[...] = jnp.where(iota((r, c), 1) // 2 == iota((r, c), 0), 0.25, 0.0).astype(BF16)
    r, c = up.shape
    up[...] = jnp.where(iota((r, c), 0) // 2 == iota((r, c), 1), 1.0, 0.0).astype(BF16)
    r, c = right.shape
    right[...] = jnp.where(iota((r, c), 0) // 2 == iota((r, c), 1), 1.0, 0.0).astype(BF16)
    r, c = left.shape
    left[...] = jnp.where(iota((r, c), 1) // 2 == iota((r, c), 0), 1.0, 0.0).astype(BF16)

    def restrict(x):
        r, c = x.shape
        paired = dot2(x, down[:r // 2, :r], left=True)
        return dot2(paired, right[:c, :c // 2])

    def prolong(x):
        r, c = x.shape
        tall = dot2(x, up[:2 * r, :r], left=True)
        return dot2(tall, left[:c, :2 * c])

    def chunks(d, body):
        rows = sizes[d][0]

        def run(index, carry):
            body(pl.multiple_of(index * step, step))
            return carry

        lax.fori_loop(0, rows // step, run, 0, unroll=2)

    def neighbours(ref, at):
        now = ref[pl.ds(at + step, step), :]
        before = ref[pl.ds(at, step), :]
        after = ref[pl.ds(at + 2 * step, step), :]
        above, below = shift_rows(before, now, after)
        cols = now.shape[1]
        return now, above, below, pltpu.roll(now, 1, 1), pltpu.roll(now, cols - 1, 1)

    for d in range(LEVELS):
        m = lev[d]
        rows, cols = sizes[d]
        zero = jnp.zeros((step, cols), F32)
        for name in ("visc", "a", "b"):
            m[name][0:step, :] = zero
            m[name][rows + step:rows + 2 * step, :] = zero
        m["visc"][step:rows + step, :] = visc[...] if d == 0 else restrict(
            lev[d - 1]["visc"][step:2 * rows + step, :])
        if d == 0:
            m["fric"][...] = fric[...]
        else:
            m["fric"][...] = restrict(lev[d - 1]["fric"][...])
        halo = ext // 3 >> d
        low = jnp.where(jnp.logical_and(core == 0, b == 0), halo, 0)
        high = jnp.where(jnp.logical_and(core == 1, b == n_blk - 1), rows - halo, rows)
        scale = 0.5 * 0.25 ** d

        def faces(at, m=m, cols=cols, low=low, high=high, scale=scale):
            now, above, below, west, east = neighbours(m["visc"], at)
            col = iota(now.shape, 1)
            fe = scale * (now + below)
            fw = scale * (now + above)
            fn = scale * (now + jnp.where(col == cols - 1, 0.0, east))
            fs = scale * (now + jnp.where(col == 0, 0.0, west))
            here = pl.ds(at, step)
            diag = fe + fw + fn + fs + m["fric"][here, :]
            row = iota(now.shape, 0) + at
            inside = jnp.logical_and(row >= low, row < high)
            m["d"][here, :] = diag
            m["i"][here, :] = jnp.where(inside, omega / diag, 0.0)
            m["e"][here, :] = fe
            m["w"][here, :] = fw
            m["n"][here, :] = jnp.where(col == cols - 1, 0.0, fn)
            m["s"][here, :] = jnp.where(col == 0, 0.0, fs)

        chunks(d, faces)

    def flux(m, ref, at):
        now, above, below, west, east = neighbours(ref, at)
        here = pl.ds(at, step)
        total = (m["f"][here, :] + m["e"][here, :] * below + m["w"][here, :] * above
                 + m["n"][here, :] * east + m["s"][here, :] * west)
        return now, total

    def sweep(d, old, new):
        m = lev[d]

        def body(at):
            now, total = flux(m, m[old], at)
            m[new][pl.ds(at + step, step), :] = (1.0 - omega) * now + m["i"][pl.ds(at, step), :] * total

        chunks(d, body)

    def first(d, new):
        m = lev[d]

        def body(at):
            here = pl.ds(at, step)
            m[new][pl.ds(at + step, step), :] = m["i"][here, :] * m["f"][here, :]

        chunks(d, body)

    def residual(d, old, new):
        m = lev[d]

        def body(at):
            now, total = flux(m, m[old], at)
            m[new][pl.ds(at + step, step), :] = total - m["d"][pl.ds(at, step), :] * now

        chunks(d, body)

    def vcycle(d, zero):
        m = lev[d]
        rows, cols = sizes[d]
        sweeps = COARSE_SWEEPS if d == LEVELS - 1 else SMOOTH_SWEEPS
        names = ("a", "b") if sweeps % 2 == 0 else ("b", "a")
        for index in range(sweeps):
            old, new = ("a", "b") if index % 2 == 0 else ("b", "a")
            if index == 0 and zero:
                first(d, new)
            else:
                sweep(d, old, new)
        if d == LEVELS - 1:
            return
        residual(d, "a", "b")
        lev[d + 1]["f"][...] = restrict(m["b"][step:rows + step, :])
        vcycle(d + 1, True)
        m["a"][step:rows + step, :] += prolong(lev[d + 1]["a"][step:rows // 2 + step, :])
        for index in range(SMOOTH_SWEEPS):
            old, new = ("a", "b") if index % 2 == 0 else ("b", "a")
            sweep(d, old, new)

    lev[0]["f"][...] = source[...]
    for cycle_index in range(CYCLES):
        vcycle(0, cycle_index == 0)
    third = ext // 3
    out[...] = lev[0]["a"][third + step:2 * third + step, :]


def params(collective=None):
    if collective is None:
        return pltpu.CompilerParams(vmem_limit_bytes=LIMIT)
    return pltpu.CompilerParams(
        vmem_limit_bytes=LIMIT, collective_id=collective, has_side_effects=True)


def shards(n_grp, n_blk, temp, uvel, vvel, couple_col, couple_cell, cavity, thickness, viscosity,
           friction, drive):
    levels, orows, ocols = temp.shape
    rows, cols = thickness.shape
    half = rows // 2
    count = couple_col.shape[-1]
    col = couple_col.reshape(1, count)
    cell = couple_cell.reshape(1, count)
    cav = cavity.reshape(1, count)
    row_edge = jnp.stack([jnp.stack([temp[:, 0, :], uvel[:, 0, :]]),
                          jnp.stack([temp[:, -1, :], uvel[:, -1, :]])])
    col_edge = jnp.stack([jnp.stack([temp[:, :, 0], vvel[:, :, 0]]),
                          jnp.stack([temp[:, :, -1], vvel[:, :, -1]])])

    def shape(*dims):
        return jax.ShapeDtypeStruct(dims, F32)

    part, drafts, top, visc, fric, row_in, col_in = pl.pallas_call(
        functools.partial(couple_kernel, n_grp, n_blk),
        out_shape=(shape(rows, cols), shape(n_blk, 1, count), shape(1, count),
                   shape(3 * half, cols), shape(3 * half, cols),
                   shape(2, 2, levels, ocols), shape(2, 2, levels, orows)),
        in_specs=[VM] * 9,
        out_specs=(VM,) * 7,
        scratch_shapes=[
            pltpu.VMEM((n_blk - 1, 1, count), jnp.int32),
            pltpu.VMEM((n_blk - 1, 1, count), jnp.int32),
            pltpu.VMEM((n_blk, 1, count), F32),
            pltpu.VMEM((3 * rows, cols), F32),
            pltpu.SemaphoreType.DMA((n_blk - 1, 3)),
            pltpu.SemaphoreType.DMA((n_blk - 1, 3)),
            pltpu.SemaphoreType.DMA((6,)),
            pltpu.SemaphoreType.DMA((6,)),
        ],
        compiler_params=params(0),
        name="couple",
    )(temp[0], col, cell, cav, thickness, viscosity, friction, row_edge, col_edge)

    nz = n_grp // 2
    source, draft = pl.pallas_call(
        functools.partial(reduce_kernel, n_grp, n_blk),
        out_shape=(shape(3 * half, cols), shape(1, count)),
        in_specs=[VM] * 3,
        out_specs=(VM,) * 2,
        scratch_shapes=[
            pltpu.VMEM((half, cols), F32),
            pltpu.VMEM((half, cols), F32),
            pltpu.VMEM((nz - 1, half // nz, cols), F32),
            pltpu.VMEM((n_blk - 1, 1, count), F32),
            pltpu.SemaphoreType.DMA((2 * nz + 2,)),
            pltpu.SemaphoreType.DMA((2 * nz + 2,)),
            pltpu.SemaphoreType.DMA((n_blk - 1,)),
            pltpu.SemaphoreType.DMA((n_blk - 1,)),
        ],
        compiler_params=params(1),
        name="reduce",
    )(part, drive, drafts)

    ext = 3 * half
    scratch = []
    for depth in range(LEVELS):
        r, c = ext >> depth, cols >> depth
        tall, flat = pltpu.VMEM((r + 16, c), F32), pltpu.VMEM((r, c), F32)
        scratch += [tall, flat, flat, tall, tall] + [flat] * 6
    scratch += [pltpu.VMEM((ext // 2, ext), BF16), pltpu.VMEM((cols, cols // 2), BF16),
                pltpu.VMEM((ext, ext // 2), BF16), pltpu.VMEM((cols // 2, cols), BF16)]
    block = pl.pallas_call(
        functools.partial(solve_kernel, n_blk),
        out_shape=shape(half, cols),
        in_specs=[VM] * 3,
        out_specs=VM,
        scratch_shapes=scratch,
        compiler_params=params(),
        name="solve",
    )(source, visc, fric)

    velocity = pl.pallas_call(
        swap_kernel,
        out_shape=shape(rows, cols),
        in_specs=[VM],
        out_specs=VM,
        scratch_shapes=[pltpu.SemaphoreType.DMA, pltpu.SemaphoreType.DMA],
        compiler_params=params(2),
        name="swap",
    )(block)

    temp_new = pl.pallas_call(
        functools.partial(ocean_kernel, n_grp, n_blk),
        out_shape=shape(levels, orows, ocols),
        in_specs=[VM] * 9,
        out_specs=VM,
        compiler_params=params(),
        name="ocean",
    )(temp, uvel, vvel, row_in, col_in[..., None], col, cav, top, draft)
    return (temp_new, velocity)


def solution(mesh):
    sizes = dict(mesh.shape)
    return jax.shard_map(
        functools.partial(shards, sizes["grp"], sizes["blk"]),
        mesh=mesh,
        in_specs=(
            P(None, "grp", "blk"),
            P(None, "grp", "blk"),
            P(None, "grp", "blk"),
            P("grp", "blk", None),
            P("grp", "blk", None),
            P("grp", "blk", None),
            P("blk", None),
            P("blk", None),
            P("blk", None),
            P("blk", None),
        ),
        out_specs=(P(None, "grp", "blk"), P("blk", None)),
        check_vma=False,
    )
```

time: 533 us -> 92.9 us (0.17)
  the two profiles are of different devices: /device:TPU:12 before, /device:TPU:0 now
where the time goes in v1:
time: 92.9 us; the launch traced here: 91.6 us
  Pallas kernels  82.1 us (88%)
  local copies, waits for them, and re-layouts  7.62 us (8%)
  other arithmetic  1.24 us (1%)
    pallas_call x1, Pallas kernels, shards(): pl.pallas_call(functools.partial(solve_kernel, n_blk), out_shape=shape(ha...  28.8 us
    pallas_call x1, Pallas kernels, shards(): pl.pallas_call(functools.partial(couple_kernel, n_grp, n_blk), out_shape=...  22.1 us
    pallas_call x1, Pallas kernels, shards(): pl.pallas_call(functools.partial(reduce_kernel, n_grp, n_blk), out_shape=...  18.7 us
    pallas_call x1, Pallas kernels, shards(): pl.pallas_call(swap_kernel, out_shape=shape(rows, cols), in_specs=[VM], o...  9.47 us
    pallas_call x1, Pallas kernels, shards(): pl.pallas_call(functools.partial(ocean_kernel, n_grp, n_blk), out_shape=s...  3.08 us
    unnamed x11, local copies, waits for them, and re-layouts  2.01 us

profile of v1, /device:TPU:0, one launch (start us, length us, event | category | flops | bytes accessed | tf_op | source)
XLA Modules:
  0.0 91.6 jit_solution(6740245245499669806)
XLA Ops:
  0.6 0.8 fusion.3
  1.4 0.8 fusion.2
  2.2 0.6 pad_maximum_fusion.row_edge
  2.8 1.4 %slice_bitcast_fusion.temp0 = f32[64,128]{1,0:T(8,128)} fusion(f32[8,64,128]{2,1,0:T(8,128)} %temp.1), kind=kLoop, calls=%fused_computation | loop fusion | bytes 65536 | tf_op jit(solution)/shard_map/squeeze | solution.py:552
  4.2 1.2 %fusion.1 = (f32[8,64,1]{2,1,0:T(8,128)S(1)}, f32[8,64,1]{2,1,0:T(8,128)S(1)}) fusion(f32[8,64,128]{2,1,0:T(8,128)} %vvel.1), kind=kLoop, calls=%fused_computation.8 | loop fusion | bytes 8192 | tf_op jit(solution)/shard_map/slice | solution.py:527
  5.3 0.0 copy-start
  5.4 0.1 copy.34
  5.5 0.1 copy.36
  5.6 0.7 copy-done
  6.3 0.1 fusion
  6.4 0.1 copy.33
  6.6 0.1 copy.35
  6.7 0.6 pad_maximum_fusion.1.col_edge
  7.3 22.1 %couple.1 = (f32[128,1024]{1,0:T(8,128)}, f32[4,1,2048]{2,1,0:T(1,128)}, f32[1,2048]{1,0:T(1,128)}, f32[192,1024]{1,0:T(8,128)}, f32[192,1024]{1,0:T(8,128)}, /*...) custom-call(f32[64,128]{1,0:T(8,128)} %slice_bitcast_fusion.temp0, s32[1,2048]{1,0:T(1,128)} %bitcast.30, ...), custom_call_target="tpu_custom_call" | custom-call | tf_op jit(solution)/shard_map/couple/pallas_call | solution.py:533
  29.4 18.7 %reduce.1 = (f32[192,1024]{1,0:T(8,128)}, f32[1,2048]{1,0:T(1,128)}) custom-call(f32[128,1024]{1,0:T(8,128)} %get-tuple-element.14.part, f32[128,1024]{1,0:T(8,128)} %drive.1, f32[4,1,2048]{2,1,0:T(1,128)} %get-tuple-element.15.drafts), custom_call_target="tpu_custom_call" | custom-call | tf_op jit(solution)/shard_map/reduce/pallas_call | solution.py:555
  48.1 28.8 %solve.1.block = f32[64,1024]{1,0:T(8,128)} custom-call(f32[192,1024]{1,0:T(8,128)} %get-tuple-element.17.source, f32[192,1024]{1,0:T(8,128)} %get-tuple-element.18.visc, f32[192,1024]{1,0:T(8,128)} %get-tuple-element.19.fric), custom_call_target="tpu_custom_call" | custom-call | tf_op jit(solution)/shard_map/solve/pallas_call | solution.py:582
  76.9 0.0 copy-start.2
  76.9 9.5 %swap.1 = f32[128,1024]{1,0:T(8,128)} custom-call(f32[64,1024]{1,0:T(8,128)} %solve.1.block), custom_call_target="tpu_custom_call" | custom-call | tf_op jit(solution)/shard_map/swap/pallas_call | solution.py:592
  86.4 0.0 copy-done.2
  86.4 1.4 %copy.28.col_edge = f32[2,2,8,64,1]{4,3,2,1,0:T(8,128)} copy(f32[2,2,8,64,1]{3,2,1,0,4:T(8,128)S(1)} %bitcast.34) | data formatting | bytes 16384 | tf_op jit(solution)/shard_map/broadcast_in_dim | solution.py:609
  87.8 0.0 copy-start.1
  87.8 3.1 %ocean.1 = f32[8,64,128]{2,1,0:T(8,128)} custom-call(f32[8,64,128]{2,1,0:T(8,128)} %temp.1, f32[8,64,128]{2,1,0:T(8,128)} %uvel.1, f32[8,64,128]{2,1,0:T(8,128)} %vvel.1, f32[2,2,8,128]{3,2,1,0:T(8,128)} %get-tuple-element.11.row_edge, f32[2,2,8,64,1]{4,3,2,1,0:T(8,128)} %copy.28.col_edge, s32[1,2048]{1,0:T(1,128)} %bitcast.31, s32[1,2048]{1,0:T(1,128)} %bitcast.33, ...), custom_call_target="tpu_custom_call" | custom-call | tf_op jit(solution)/shard_map/ocean/pallas_call | solution.py:602
  90.8 0.0 copy-done.1
  90.8 0.8 copy.38
  (2 shorter events, 0.0 us)
Async XLA Ops:
  5.3 1.0 %copy-start = (f32[8,64,128]{2,1,0:T(8,128)S(1)}, f32[8,64,128]{2,1,0:T(8,128)}, u32[]{:S(2)}) copy-start(f32[8,64,128]{2,1,0:T(8,128)} %temp.1) | copy-start | bytes 786436
  76.9 9.5 %copy-start.2 = (f32[2,2,8,64]{3,2,1,0:T(8,128)S(1)}, f32[2,2,8,64]{3,2,1,0:T(8,128)}, u32[]{:S(2)}) copy-start(f32[2,2,8,64]{3,2,1,0:T(8,128)} %get-tuple-element.12) | copy-start | bytes 24580
  87.8 3.1 %copy-start.1 = (f32[128,1024]{1,0:T(8,128)S(1)}, f32[128,1024]{1,0:T(8,128)}, u32[]{:S(2)}) copy-start(f32[128,1024]{1,0:T(8,128)} %swap.1) | copy-start | bytes 1572868

commit v2 on v0

v2 whole, which is shorter than its diff:
```python
import functools

import jax
import jax.numpy as jnp
from jax import lax
from jax.experimental import pallas as pl
from jax.experimental.pallas import tpu as pltpu
from jax.sharding import PartitionSpec as P

LEVELS = 3
SMOOTH_SWEEPS = 2
COARSE_SWEEPS = 4
CYCLES = 2

omega = 0.8
kappa = 0.1
vertical_mix = 0.2
melt_rate = 0.5

MESH = pl.DeviceIdType.MESH
VM = pl.BlockSpec(memory_space=pltpu.VMEM)
LIMIT = 56 * 1024 * 1024
F32 = jnp.float32
BF16 = jnp.bfloat16


def split(x):
    high = x.astype(BF16).astype(F32)
    return high, x - high


def dot2(x, one, left=False):
    out = None
    for part in split(x):
        part = part.astype(BF16)
        term = jnp.dot(one, part, preferred_element_type=F32) if left else jnp.dot(
            part, one, preferred_element_type=F32)
        out = term if out is None else out + term
    return out


def nt(a, b):
    return lax.dot_general(a, b, (((1,), (1,)), ((), ())), preferred_element_type=F32)


def iota(shape, dim):
    return lax.broadcasted_iota(jnp.int32, shape, dim)


def remote(src, dst, send, recv, device):
    return pltpu.make_async_remote_copy(
        src_ref=src, dst_ref=dst, send_sem=send, recv_sem=recv, device_id=device,
        device_id_type=MESH)


def ocean(n_grp, n_blk, g, b, temp, uvel, vvel, row_edge, col_edge, col, melt, out):
    levels, rows, cols = temp.shape
    count = col.shape[1]
    ids = col[...]
    row = ids // cols
    lane = ids - row * cols
    hit = iota((rows, count), 0) == row
    pick = (iota((cols, count), 0) == lane).astype(F32).astype(BF16)
    high, low = split(melt)
    surface = nt(jnp.where(hit, high, 0.0).astype(BF16), pick)
    surface = surface + nt(jnp.where(hit, low, 0.0).astype(BF16), pick)

    west_in = (g > 0).astype(F32)
    east_in = (g < n_grp - 1).astype(F32)
    south_in = (b > 0).astype(F32)
    north_in = (b < n_blk - 1).astype(F32)
    at_row = iota((rows, cols), 0)
    at_col = iota((rows, cols), 1)

    def four(x, which, rowwise, colwise, k):
        found = []
        if rowwise:
            low = row_edge[0, which, k:k + 1, :] * west_in
            high = row_edge[1, which, k:k + 1, :] * east_in
            found.append(jnp.where(at_row == rows - 1, high, pltpu.roll(x, rows - 1, 0)))
            found.append(jnp.where(at_row == 0, low, pltpu.roll(x, 1, 0)))
        if colwise:
            lane = which * levels + k
            low = col_edge[0, :, lane:lane + 1] * south_in
            high = col_edge[1, :, lane:lane + 1] * north_in
            found.append(jnp.where(at_col == cols - 1, high, pltpu.roll(x, cols - 1, 1)))
            found.append(jnp.where(at_col == 0, low, pltpu.roll(x, 1, 1)))
        return found

    for k in range(levels):
        t = temp[k]
        u = uvel[k]
        v = vvel[k]
        te, tw, tn, ts = four(t, 0, True, True, k)
        ue, uw = four(u, 1, True, False, k)
        vn, vs = four(v, 1, False, True, k)
        ue = 0.5 * (u + ue)
        uw = 0.5 * (u + uw)
        vn = 0.5 * (v + vn)
        vs = 0.5 * (v + vs)
        flux_east = jnp.maximum(ue, 0.0) * t + jnp.minimum(ue, 0.0) * te
        flux_west = jnp.maximum(uw, 0.0) * tw + jnp.minimum(uw, 0.0) * t
        flux_north = jnp.maximum(vn, 0.0) * t + jnp.minimum(vn, 0.0) * tn
        flux_south = jnp.maximum(vs, 0.0) * ts + jnp.minimum(vs, 0.0) * t
        laplace = te + tw + tn + ts - 4.0 * t
        vert = jnp.zeros_like(t)
        if k + 1 < levels:
            vert = vert + (temp[k + 1] - t)
        if k > 0:
            vert = vert - (t - temp[k - 1])
        new = (t + flux_west - flux_east + flux_south - flux_north + kappa * laplace
               + vertical_mix * vert)
        if k == 0:
            new = new - melt_rate * surface
        out[k] = new


def shift_rows(before, now, after):
    rows = now.shape[0]
    at = iota(now.shape, 0)
    above = jnp.where(at == 0, pltpu.roll(before, 1, 0), pltpu.roll(now, 1, 0))
    below = jnp.where(at == rows - 1, pltpu.roll(after, rows - 1, 0), pltpu.roll(now, rows - 1, 0))
    return above, below


def multigrid(n_blk, core, b, scratch):
    step = 8
    ext, wide = scratch[1].shape
    sizes = [(ext >> d, wide >> d) for d in range(LEVELS)]
    names = ("visc", "fric", "f", "a", "b", "e", "w", "n", "s", "d", "i")
    lev = [dict(zip(names, scratch[d * len(names):(d + 1) * len(names)])) for d in range(LEVELS)]
    down, right, up, left = scratch[LEVELS * len(names):]

    def matrices():
        r, c = down.shape
        down[...] = jnp.where(iota((r, c), 1) // 2 == iota((r, c), 0), 0.25, 0.0).astype(BF16)
        r, c = up.shape
        up[...] = jnp.where(iota((r, c), 0) // 2 == iota((r, c), 1), 1.0, 0.0).astype(BF16)
        r, c = right.shape
        right[...] = jnp.where(iota((r, c), 0) // 2 == iota((r, c), 1), 1.0, 0.0).astype(BF16)
        r, c = left.shape
        left[...] = jnp.where(iota((r, c), 1) // 2 == iota((r, c), 0), 1.0, 0.0).astype(BF16)

    def restrict(x):
        r, c = x.shape
        paired = dot2(x, down[:r // 2, :r], left=True)
        return dot2(paired, right[:c, :c // 2])

    def prolong(x):
        r, c = x.shape
        tall = dot2(x, up[:2 * r, :r], left=True)
        return dot2(tall, left[:c, :2 * c])

    def chunks(d, body, trim=0):
        rows = sizes[d][0]
        low = (trim >> d) // step
        count = rows // step - 2 * low

        def run(index, carry):
            body(pl.multiple_of((index + low) * step, step))
            return carry

        lax.fori_loop(0, count, run, 0, unroll=4 if count % 4 == 0 else 2)

    def neighbours(ref, at):
        now = ref[pl.ds(at + step, step), :]
        before = ref[pl.ds(at, step), :]
        after = ref[pl.ds(at + 2 * step, step), :]
        above, below = shift_rows(before, now, after)
        cols = now.shape[1]
        return now, above, below, pltpu.roll(now, 1, 1), pltpu.roll(now, cols - 1, 1)

    def coefficients():
        for d in range(LEVELS):
            m = lev[d]
            rows, cols = sizes[d]
            zero = jnp.zeros((step, cols), F32)
            for name in ("visc", "a", "b"):
                m[name][0:step, :] = zero
                m[name][rows + step:rows + 2 * step, :] = zero
            if d > 0:
                m["visc"][step:rows + step, :] = restrict(lev[d - 1]["visc"][step:2 * rows + step, :])
                m["fric"][...] = restrict(lev[d - 1]["fric"][...])
            halo = ext // 3 >> d
            low = jnp.where(jnp.logical_and(core == 0, b == 0), halo, 0)
            high = jnp.where(jnp.logical_and(core == 1, b == n_blk - 1), rows - halo, rows)
            scale = 0.5 * 0.25 ** d

            def faces(at, m=m, cols=cols, low=low, high=high, scale=scale):
                now, above, below, west, east = neighbours(m["visc"], at)
                col = iota(now.shape, 1)
                fe = scale * (now + below)
                fw = scale * (now + above)
                fn = scale * (now + jnp.where(col == cols - 1, 0.0, east))
                fs = scale * (now + jnp.where(col == 0, 0.0, west))
                here = pl.ds(at, step)
                diag = fe + fw + fn + fs + m["fric"][here, :]
                row = iota(now.shape, 0) + at
                inside = jnp.logical_and(row >= low, row < high)
                m["d"][here, :] = diag
                m["i"][here, :] = jnp.where(inside, omega / diag, 0.0)
                m["e"][here, :] = fe
                m["w"][here, :] = fw
                m["n"][here, :] = jnp.where(col == cols - 1, 0.0, fn)
                m["s"][here, :] = jnp.where(col == 0, 0.0, fs)

            chunks(d, faces)

    def flux(m, ref, at):
        now, above, below, west, east = neighbours(ref, at)
        here = pl.ds(at, step)
        total = (m["f"][here, :] + m["e"][here, :] * below + m["w"][here, :] * above
                 + m["n"][here, :] * east + m["s"][here, :] * west)
        return now, total

    def sweep(d, old, new, trim):
        m = lev[d]

        def body(at):
            now, total = flux(m, m[old], at)
            m[new][pl.ds(at + step, step), :] = (1.0 - omega) * now + m["i"][pl.ds(at, step), :] * total

        chunks(d, body, trim)

    def first(d, new, trim):
        m = lev[d]

        def body(at):
            here = pl.ds(at, step)
            m[new][pl.ds(at + step, step), :] = m["i"][here, :] * m["f"][here, :]

        chunks(d, body, trim)

    def residual(d, old, new, trim):
        m = lev[d]

        def body(at):
            now, total = flux(m, m[old], at)
            m[new][pl.ds(at + step, step), :] = total - m["d"][pl.ds(at, step), :] * now

        chunks(d, body, trim)

    def vcycle(d, zero, trim, after):
        m = lev[d]
        rows, cols = sizes[d]
        sweeps = COARSE_SWEEPS if d == LEVELS - 1 else SMOOTH_SWEEPS
        for index in range(sweeps):
            old, new = ("a", "b") if index % 2 == 0 else ("b", "a")
            if index == 0 and zero:
                first(d, new, trim)
            else:
                sweep(d, old, new, trim)
        if d == LEVELS - 1:
            return
        residual(d, "a", "b", trim)
        low, high = trim >> d, rows - (trim >> d)
        lev[d + 1]["f"][low // 2:high // 2, :] = restrict(m["b"][low + step:high + step, :])
        vcycle(d + 1, True, trim, trim)
        m["a"][low + step:high + step, :] += prolong(
            lev[d + 1]["a"][low // 2 + step:high // 2 + step, :])
        for index in range(SMOOTH_SWEEPS):
            old, new = ("a", "b") if index % 2 == 0 else ("b", "a")
            sweep(d, old, new, after)

    def cycles():
        inner = ext // 6
        for cycle_index in range(CYCLES):
            vcycle(0, cycle_index == 0, 0 if cycle_index < CYCLES - 1 else inner, inner)

    return lev[0], matrices, coefficients, cycles


def step_kernel(n_grp, n_blk, temp, uvel, vvel, col, cell, cav, thick, visc, fric, drive,
                temp_out, vel_out, ent_cell, ent_cav, ent_w, acc, drafts, dback, row_edge,
                col_edge, row_in, col_in, part, near, pair, far, esem_s, esem_r, hsem_s, hsem_r,
                bsem_s, bsem_r, zsem_s, zsem_r, gsem_s, gsem_r, psem_s, psem_r, osem_s, osem_r,
                sem_s, sem_r, *scratch):
    g = lax.axis_index("grp")
    b = lax.axis_index("blk")
    core = lax.rem(g, 2)
    z = g // 2
    nz = n_grp // 2
    rows, cols = thick.shape
    half = rows // 2
    size = half // nz
    count = cell.shape[1]
    levels, ocean_rows, ocean_cols = temp.shape
    up_g, dn_g = lax.rem(g + 1, n_grp), lax.rem(g + n_grp - 1, n_grp)
    up_b, dn_b = lax.rem(b + 1, n_blk), lax.rem(b + n_blk - 1, n_blk)
    partner = g + 1 - 2 * core
    outer = (partner, lax.rem(b + n_blk - 1 + 2 * core, n_blk))
    fine, matrices, coefficients, cycles = multigrid(n_blk, core, b, scratch)
    pad = 8

    def aligned(x):
        return pl.multiple_of(x, 8)

    barrier = pltpu.get_barrier_semaphore()
    peers = [(g, lax.rem(b + k, n_blk)) for k in range(1, n_blk)]
    bpeers = [(g, lax.rem(b + n_blk - k, n_blk)) for k in range(1, n_blk)]
    zpeers = [(lax.rem(g + 2 * k, n_grp), b) for k in range(1, nz)]
    greet = peers + [(up_g, b), (dn_g, b), (partner, b), outer] + zpeers
    for device in greet:
        pl.semaphore_signal(barrier, inc=1, device_id=device, device_id_type=MESH)
    at_lane = iota((ocean_rows, ocean_cols), 1)
    for side in range(2):
        edge = jnp.zeros((ocean_rows, ocean_cols), F32)
        r, c = (0, 0) if side == 0 else (ocean_rows - 1, ocean_cols - 1)
        for k in range(levels):
            row_edge[side, 0, k:k + 1, :] = temp[k, r:r + 1, :]
            row_edge[side, 1, k:k + 1, :] = uvel[k, r:r + 1, :]
            for which, ref in enumerate((temp, vvel)):
                lane = which * levels + k
                moved = pltpu.roll(ref[k], (lane - c) % ocean_cols, 1)
                edge = jnp.where(at_lane == lane, moved, edge)
        col_edge[side] = edge
    pl.semaphore_wait(barrier, len(greet))

    ent = []
    for k in range(1, n_blk):
        target = peers[k - 1]
        trio = [
            remote(cell, ent_cell.at[k - 1], esem_s.at[k - 1, 0], esem_r.at[k - 1, 0], target),
            remote(cav, ent_cav.at[k - 1], esem_s.at[k - 1, 1], esem_r.at[k - 1, 1], target),
            remote(ent_w.at[0], ent_w.at[k], esem_s.at[k - 1, 2], esem_r.at[k - 1, 2], target),
        ]
        trio[0].start()
        trio[1].start()
        ent.append(trio)

    ids = col[...]
    ocean_row = ids // ocean_cols
    ocean_lane = ids - ocean_row * ocean_cols
    pick = (iota((ocean_cols, count), 0) == ocean_lane).astype(F32).astype(BF16)
    surface = temp[0]
    rest = split(split(surface)[1])[1]
    wide = dot2(surface, pick) + jnp.dot(rest.astype(BF16), pick, preferred_element_type=F32)
    top = jnp.sum(jnp.where(iota((ocean_rows, count), 0) == ocean_row, wide, 0.0), axis=0,
                  keepdims=True)
    ent_w[0] = cav[...].astype(F32) * melt_rate * (top + 0.5)
    for trio in ent:
        trio[2].start()

    edges = [
        remote(row_edge.at[1], row_in.at[0], hsem_s.at[0], hsem_r.at[0], (up_g, b)),
        remote(row_edge.at[0], row_in.at[1], hsem_s.at[1], hsem_r.at[1], (dn_g, b)),
        remote(col_edge.at[1], col_in.at[0], hsem_s.at[2], hsem_r.at[2], (g, up_b)),
        remote(col_edge.at[0], col_in.at[1], hsem_s.at[3], hsem_r.at[3], (g, dn_b)),
    ]
    for copy in edges:
        copy.start()
    own = aligned((1 - core) * half)
    halo = aligned(core * 2 * half)
    target = (g, lax.rem(b + n_blk + 1 - 2 * core, n_blk))
    does = jnp.where(core == 0, b < n_blk - 1, b > 0)
    gets = jnp.where(core == 0, b > 0, b < n_blk - 1)
    ice = [
        remote(visc.at[pl.ds(own, half)], fine["visc"].at[pl.ds(halo + pad, half)], hsem_s.at[4],
               hsem_r.at[4], target),
        remote(fric.at[pl.ds(own, half)], fine["fric"].at[pl.ds(halo, half)], hsem_s.at[5],
               hsem_r.at[5], target),
    ]

    @pl.when(does)
    def _():
        for copy in ice:
            copy.start()

    fine["visc"][pl.ds(own + pad, 2 * half), :] = visc[...]
    fine["fric"][pl.ds(own, 2 * half), :] = fric[...]

    @pl.when(jnp.logical_not(gets))
    def _():
        fine["visc"][pl.ds(halo + pad, half), :] = jnp.zeros((half, cols), F32)
        fine["fric"][pl.ds(halo, half), :] = jnp.ones((half, cols), F32)

    high, low = split(thick[...])
    thick2 = jnp.concatenate([high, low], axis=0).astype(BF16)
    acc[...] = jnp.zeros_like(acc)
    chunk = min(512, count)
    for k in range(n_blk):
        if k > 0:
            for copy in ent[k - 1]:
                copy.wait_recv()
        cells_ref = cell if k == 0 else ent_cell.at[k - 1]
        cav_ref = cav if k == 0 else ent_cav.at[k - 1]

        for piece in range(count // chunk):
            at = slice(piece * chunk, (piece + 1) * chunk)
            cells = cells_ref[:, at]
            grid_row = cells // cols
            lane = cells - grid_row * cols
            hit = iota((rows, chunk), 0) == grid_row - b * rows
            pick = (iota((cols, chunk), 0) == lane).astype(F32).astype(BF16)
            found = jnp.dot(thick2, pick, preferred_element_type=F32)
            draft = jnp.sum(jnp.where(hit, found[:rows] + found[rows:], 0.0), axis=0, keepdims=True)
            drafts[k, :, at] = draft
            melt = ent_w[k, :, at] + cav_ref[:, at].astype(F32) * (0.5 * melt_rate) * draft
            m_high, m_low = split(melt)
            spread = jnp.concatenate(
                [jnp.where(hit, m_high, 0.0).astype(BF16), jnp.where(hit, m_low, 0.0).astype(BF16)],
                axis=0)
            acc[...] += nt(spread, pick)

    part[...] = acc[:rows] + acc[rows:]

    give = aligned((1 - core) * half)
    keep = aligned(core * half)
    first = remote(part.at[pl.ds(give, half)], pair, sem_s.at[0], sem_r.at[0], (partner, b))
    first.start()
    back = [
        remote(drafts.at[k], dback.at[k - 1], bsem_s.at[k - 1], bsem_r.at[k - 1], bpeers[k - 1])
        for k in range(1, n_blk)
    ]
    for copy in back:
        copy.start()
    matrices()
    first.wait_recv()
    near[...] = part[pl.ds(keep, half), :] + pair[...]

    scatter = []
    for k in range(1, nz):
        to = lax.rem(z + k, nz)
        copy = remote(near.at[pl.ds(aligned(to * size), size)], far.at[k - 1],
                      zsem_s.at[k - 1], zsem_r.at[k - 1], zpeers[k - 1])
        copy.start()
        scatter.append(copy)

    @pl.when(gets)
    def _():
        for copy in ice:
            copy.wait_recv()

    coefficients()

    source = fine["f"]
    mine = aligned(z * size)
    total = near[pl.ds(mine, size), :] + drive[pl.ds(aligned(core * half + z * size), size), :]
    for k in range(1, nz):
        scatter[k - 1].wait_recv()
        total = total + far[k - 1]
    source[pl.ds(aligned(half + z * size), size), :] = total

    there = core * 2 * half
    away = (1 - core) * 2 * half
    out_does = jnp.where(core == 0, b > 0, b < n_blk - 1)
    spread, swaps, outs = [], [], []
    for k in range(1, nz):
        block = source.at[pl.ds(aligned(half + z * size), size)]
        copy = remote(block, block, gsem_s.at[k - 1], gsem_r.at[k - 1], zpeers[k - 1])
        copy.start()
        spread.append(copy)

    def forward(k):
        at = lax.rem(z + nz - k, nz) * size
        block = source.at[pl.ds(aligned(half + at), size)]
        swap = remote(block, source.at[pl.ds(aligned(there + at), size)], psem_s.at[k],
                      psem_r.at[k], (partner, b))
        out = remote(block, source.at[pl.ds(aligned(away + at), size)], osem_s.at[k],
                     osem_r.at[k], outer)
        swap.start()
        swaps.append(swap)
        outs.append(out)

        @pl.when(out_does)
        def _():
            out.start()

    forward(0)

    @pl.when(jnp.logical_not(out_does))
    def _():
        source[pl.ds(aligned(there), half), :] = jnp.zeros((half, cols), F32)

    for copy in edges:
        copy.wait()
    draft = drafts[0]
    for k in range(1, n_blk):
        back[k - 1].wait_recv()
        draft = draft + dback[k - 1]
    for k in range(1, nz):
        spread[k - 1].wait_recv()
        forward(k)

    melt = ent_w[0] + cav[...].astype(F32) * (0.5 * melt_rate) * draft
    ocean(n_grp, n_blk, g, b, temp, uvel, vvel, row_in, col_in, col, melt, temp_out)

    for copy in swaps:
        copy.wait()

    @pl.when(out_does)
    def _():
        for copy in outs:
            copy.wait()

    cycles()

    here = aligned(core * half)
    block = fine["a"].at[pl.ds(half + pad, half)]
    last = remote(block, vel_out.at[pl.ds(here, half)], sem_s.at[1], sem_r.at[1], (partner, b))
    last.start()
    vel_out[pl.ds(here, half), :] = fine["a"][half + pad:2 * half + pad, :]
    for trio in ent:
        for copy in trio:
            copy.wait_send()

    @pl.when(does)
    def _():
        for copy in ice:
            copy.wait_send()

    first.wait_send()
    for copy in back + scatter + spread:
        copy.wait_send()
    last.wait()


def shards(n_grp, n_blk, temp, uvel, vvel, couple_col, couple_cell, cavity, thickness, viscosity,
           friction, drive):
    levels, orows, ocols = temp.shape
    rows, cols = thickness.shape
    half = rows // 2
    count = couple_col.shape[-1]
    nz = n_grp // 2
    ext = 3 * half
    scratch = []
    for depth in range(LEVELS):
        r, c = ext >> depth, cols >> depth
        tall, flat = pltpu.VMEM((r + 16, c), F32), pltpu.VMEM((r, c), F32)
        scratch += [tall, flat, flat, tall, tall] + [flat] * 6
    scratch += [pltpu.VMEM((ext // 2, ext), BF16), pltpu.VMEM((cols, cols // 2), BF16),
                pltpu.VMEM((ext, ext // 2), BF16), pltpu.VMEM((cols // 2, cols), BF16)]

    def pair_of(*dims):
        return [pltpu.SemaphoreType.DMA(dims)] * 2

    return pl.pallas_call(
        functools.partial(step_kernel, n_grp, n_blk),
        out_shape=(jax.ShapeDtypeStruct((levels, orows, ocols), F32),
                   jax.ShapeDtypeStruct((rows, cols), F32)),
        in_specs=[VM] * 10,
        out_specs=(VM,) * 2,
        scratch_shapes=[
            pltpu.VMEM((n_blk - 1, 1, count), jnp.int32),
            pltpu.VMEM((n_blk - 1, 1, count), jnp.int32),
            pltpu.VMEM((n_blk, 1, count), F32),
            pltpu.VMEM((2 * rows, cols), F32),
            pltpu.VMEM((n_blk, 1, count), F32),
            pltpu.VMEM((n_blk - 1, 1, count), F32),
            pltpu.VMEM((2, 2, levels, ocols), F32),
            pltpu.VMEM((2, orows, ocols), F32),
            pltpu.VMEM((2, 2, levels, ocols), F32),
            pltpu.VMEM((2, orows, ocols), F32),
            pltpu.VMEM((rows, cols), F32),
            pltpu.VMEM((half, cols), F32),
            pltpu.VMEM((half, cols), F32),
            pltpu.VMEM((nz - 1, half // nz, cols), F32),
        ] + pair_of(n_blk - 1, 3) + pair_of(6) + pair_of(n_blk - 1) + pair_of(nz - 1)
        + pair_of(nz - 1) + pair_of(nz) + pair_of(nz) + pair_of(2) + scratch,
        compiler_params=pltpu.CompilerParams(
            vmem_limit_bytes=LIMIT, collective_id=0, has_side_effects=True),
        name="step",
    )(temp, uvel, vvel, couple_col.reshape(1, count), couple_cell.reshape(1, count),
      cavity.reshape(1, count), thickness, viscosity, friction, drive)


def solution(mesh):
    sizes = dict(mesh.shape)
    return jax.shard_map(
        functools.partial(shards, sizes["grp"], sizes["blk"]),
        mesh=mesh,
        in_specs=(
            P(None, "grp", "blk"),
            P(None, "grp", "blk"),
            P(None, "grp", "blk"),
            P("grp", "blk", None),
            P("grp", "blk", None),
            P("grp", "blk", None),
            P("blk", None),
            P("blk", None),
            P("blk", None),
            P("blk", None),
        ),
        out_specs=(P(None, "grp", "blk"), P("blk", None)),
        check_vma=False,
    )
```

time: 533 us -> 59.6 us (0.11)
  the two profiles are of different devices: /device:TPU:12 before, /device:TPU:0 now
where the time goes in v2:
time: 59.6 us; the launch traced here: 59.4 us
  Pallas kernels  56.2 us (94%)
  local copies, waits for them, and re-layouts  2.53 us (4%)
  between operations  0.65 us (1%)
    pallas_call x1, Pallas kernels, shards(): pl.pallas_call(functools.partial(step_kernel, n_grp, n_blk), out_shape=(j...  56.2 us
    unnamed x4, local copies, waits for them, and re-layouts  2.53 us

profile of v2, /device:TPU:0, one launch (start us, length us, event | category | flops | bytes accessed | tf_op | source)
XLA Modules:
  0.0 59.4 jit_solution(10566387683161622930)
XLA Ops:
  0.6 56.2 %step.1 = (f32[8,64,128]{2,1,0:T(8,128)}, f32[128,1024]{1,0:T(8,128)}) custom-call(f32[8,64,128]{2,1,0:T(8,128)} %temp.1, f32[8,64,128]{2,1,0:T(8,128)} %uvel.1, f32[8,64,128]{2,1,0:T(8,128)} %vvel.1, s32[1,2048]{1,0:T(1,128)} %bitcast.3, s32[1,2048]{1,0:T(1,128)} %bitcast.4, s32[1,2048]{1,0:T(1,128)} %bitcast.5, f32[128,1024]{1,0:T(8,128)} %thick.1, ...), custom_call_target="tpu_custom_call" | custom-call | tf_op jit(solution)/shard_map/step/pallas_call | solution.py:537
  56.9 0.0 copy-start
  56.9 1.7 %copy.14 = f32[8,64,128]{2,1,0:T(8,128)} copy(f32[8,64,128]{2,1,0:T(8,128)} %get-tuple-element.4) | data formatting | bytes 524288
  58.6 0.0 copy-done
  58.6 0.8 %copy.15 = f32[128,1024]{1,0:T(8,128)} copy(f32[128,1024]{1,0:T(8,128)S(1)} %copy-done) | data formatting | bytes 1048576
Async XLA Ops:
  56.9 1.7 %copy-start = (f32[128,1024]{1,0:T(8,128)S(1)}, f32[128,1024]{1,0:T(8,128)}, u32[]{:S(2)}) copy-start(f32[128,1024]{1,0:T(8,128)} %get-tuple-element.5) | copy-start | bytes 1572868

commit v3 on v2

--- a/solution.py
+++ b/solution.py
@@ -141,15 +141,25 @@
         r, c = left.shape
         left[...] = jnp.where(iota((r, c), 1) // 2 == iota((r, c), 0), 1.0, 0.0).astype(BF16)
 
+    def panels(x, one):
+        r, c = x.shape
+        width = one.shape[0]
+        count = c // width
+        stacked = jnp.concatenate(
+            [part[:, p * width:(p + 1) * width].astype(BF16)
+             for part in split(x) for p in range(count)], axis=0)
+        y = jnp.dot(stacked, one, preferred_element_type=F32)
+        return jnp.concatenate(
+            [y[p * r:(p + 1) * r] + y[(count + p) * r:(count + p + 1) * r] for p in range(count)],
+            axis=1)
+
     def restrict(x):
         r, c = x.shape
-        paired = dot2(x, down[:r // 2, :r], left=True)
-        return dot2(paired, right[:c, :c // 2])
+        return dot2(panels(x, right[...]), down[:r // 2, :r], left=True)
 
     def prolong(x):
         r, c = x.shape
-        tall = dot2(x, up[:2 * r, :r], left=True)
-        return dot2(tall, left[:c, :2 * c])
+        return panels(dot2(x, up[:2 * r, :r], left=True), left[...])
 
     def chunks(d, body, trim=0):
         rows = sizes[d][0]
@@ -160,7 +170,7 @@
             body(pl.multiple_of((index + low) * step, step))
             return carry
 
-        lax.fori_loop(0, count, run, 0, unroll=4 if count % 4 == 0 else 2)
+        lax.fori_loop(0, count, run, 0, unroll=count if d else 8 if count % 8 == 0 else 2)
 
     def neighbours(ref, at):
         now = ref[pl.ds(at + step, step), :]
@@ -528,8 +538,8 @@
         r, c = ext >> depth, cols >> depth
         tall, flat = pltpu.VMEM((r + 16, c), F32), pltpu.VMEM((r, c), F32)
         scratch += [tall, flat, flat, tall, tall] + [flat] * 6
-    scratch += [pltpu.VMEM((ext // 2, ext), BF16), pltpu.VMEM((cols, cols // 2), BF16),
-                pltpu.VMEM((ext, ext // 2), BF16), pltpu.VMEM((cols // 2, cols), BF16)]
+    scratch += [pltpu.VMEM((ext // 2, ext), BF16), pltpu.VMEM((256, 128), BF16),
+                pltpu.VMEM((ext, ext // 2), BF16), pltpu.VMEM((128, 256), BF16)]
 
     def pair_of(*dims):
         return [pltpu.SemaphoreType.DMA(dims)] * 2

time: 59.6 us -> 56 us (0.940)
  Pallas kernels: 56.2 us -> 52.6 us
    pallas_call x1, Pallas kernels: 56.2 us -> 52.6 us  [shards(): pl.pallas_call(functools.partial(step_kernel, n_grp, n_blk), out_shape=(j...]
where the time goes in v3:
time: 56 us; the launch traced here: 55.8 us
  Pallas kernels  52.6 us (94%)
  local copies, waits for them, and re-layouts  2.53 us (5%)
  between operations  0.65 us (1%)
    pallas_call x1, Pallas kernels, shards(): pl.pallas_call(functools.partial(step_kernel, n_grp, n_blk), out_shape=(j...  52.6 us
    unnamed x4, local copies, waits for them, and re-layouts  2.53 us

profile of v3, /device:TPU:0, one launch (start us, length us, event | category | flops | bytes accessed | tf_op | source)
XLA Modules:
  0.0 55.8 jit_solution(9335528385556623941)
XLA Ops:
  0.6 52.6 %step.1 = (f32[8,64,128]{2,1,0:T(8,128)}, f32[128,1024]{1,0:T(8,128)}) custom-call(f32[8,64,128]{2,1,0:T(8,128)} %temp.1, f32[8,64,128]{2,1,0:T(8,128)} %uvel.1, f32[8,64,128]{2,1,0:T(8,128)} %vvel.1, s32[1,2048]{1,0:T(1,128)} %bitcast.3, s32[1,2048]{1,0:T(1,128)} %bitcast.4, s32[1,2048]{1,0:T(1,128)} %bitcast.5, f32[128,1024]{1,0:T(8,128)} %thick.1, ...), custom_call_target="tpu_custom_call" | custom-call | tf_op jit(solution)/shard_map/step/pallas_call | solution.py:547
  53.3 0.0 copy-start
  53.3 1.7 %copy.14 = f32[8,64,128]{2,1,0:T(8,128)} copy(f32[8,64,128]{2,1,0:T(8,128)} %get-tuple-element.4) | data formatting | bytes 524288
  55.0 0.0 copy-done
  55.0 0.8 %copy.15 = f32[128,1024]{1,0:T(8,128)} copy(f32[128,1024]{1,0:T(8,128)S(1)} %copy-done) | data formatting | bytes 1048576
Async XLA Ops:
  53.3 1.7 %copy-start = (f32[128,1024]{1,0:T(8,128)S(1)}, f32[128,1024]{1,0:T(8,128)}, u32[]{:S(2)}) copy-start(f32[128,1024]{1,0:T(8,128)} %get-tuple-element.5) | copy-start | bytes 1572868

commit v4 on v3

--- a/solution.py
+++ b/solution.py
@@ -387,7 +387,7 @@
     high, low = split(thick[...])
     thick2 = jnp.concatenate([high, low], axis=0).astype(BF16)
     acc[...] = jnp.zeros_like(acc)
-    chunk = min(512, count)
+    chunk = min(1024, count)
     for k in range(n_blk):
         if k > 0:
             for copy in ent[k - 1]:

time: 56 us -> 54.9 us (0.980)
  Pallas kernels: 52.6 us -> 51.6 us
    pallas_call x1, Pallas kernels: 52.6 us -> 51.6 us  [shards(): pl.pallas_call(functools.partial(step_kernel, n_grp, n_blk), out_shape=(j...]
where the time goes in v4:
time: 54.9 us; the launch traced here: 54.7 us
  Pallas kernels  51.6 us (94%)
  local copies, waits for them, and re-layouts  2.53 us (5%)
  between operations  0.65 us (1%)
    pallas_call x1, Pallas kernels, shards(): pl.pallas_call(functools.partial(step_kernel, n_grp, n_blk), out_shape=(j...  51.6 us
    unnamed x4, local copies, waits for them, and re-layouts  2.53 us

profile of v4, /device:TPU:0, one launch (start us, length us, event | category | flops | bytes accessed | tf_op | source)
XLA Modules:
  0.0 54.7 jit_solution(1178325742976158639)
XLA Ops:
  0.6 51.6 %step.1 = (f32[8,64,128]{2,1,0:T(8,128)}, f32[128,1024]{1,0:T(8,128)}) custom-call(f32[8,64,128]{2,1,0:T(8,128)} %temp.1, f32[8,64,128]{2,1,0:T(8,128)} %uvel.1, f32[8,64,128]{2,1,0:T(8,128)} %vvel.1, s32[1,2048]{1,0:T(1,128)} %bitcast.3, s32[1,2048]{1,0:T(1,128)} %bitcast.4, s32[1,2048]{1,0:T(1,128)} %bitcast.5, f32[128,1024]{1,0:T(8,128)} %thick.1, ...), custom_call_target="tpu_custom_call" | custom-call | tf_op jit(solution)/shard_map/step/pallas_call | solution.py:547
  52.2 0.0 copy-start
  52.2 1.7 %copy.14 = f32[8,64,128]{2,1,0:T(8,128)} copy(f32[8,64,128]{2,1,0:T(8,128)} %get-tuple-element.4) | data formatting | bytes 524288
  53.9 0.0 copy-done
  53.9 0.8 %copy.15 = f32[128,1024]{1,0:T(8,128)} copy(f32[128,1024]{1,0:T(8,128)S(1)} %copy-done) | data formatting | bytes 1048576
Async XLA Ops:
  52.2 1.7 %copy-start = (f32[128,1024]{1,0:T(8,128)S(1)}, f32[128,1024]{1,0:T(8,128)}, u32[]{:S(2)}) copy-start(f32[128,1024]{1,0:T(8,128)} %get-tuple-element.5) | copy-start | bytes 1572868

commit v5 on v4

--- a/solution.py
+++ b/solution.py
@@ -387,7 +387,7 @@
     high, low = split(thick[...])
     thick2 = jnp.concatenate([high, low], axis=0).astype(BF16)
     acc[...] = jnp.zeros_like(acc)
-    chunk = min(1024, count)
+    chunk = min(2048, count)
     for k in range(n_blk):
         if k > 0:
             for copy in ent[k - 1]:

time: 54.9 us -> 54.1 us (0.985)
  Pallas kernels: 51.6 us -> 50.8 us
    pallas_call x1, Pallas kernels: 51.6 us -> 50.8 us  [shards(): pl.pallas_call(functools.partial(step_kernel, n_grp, n_blk), out_shape=(j...]
where the time goes in v5:
time: 54.1 us; the launch traced here: 54 us
  Pallas kernels  50.8 us (94%)
  local copies, waits for them, and re-layouts  2.53 us (5%)
  between operations  0.65 us (1%)
    pallas_call x1, Pallas kernels, shards(): pl.pallas_call(functools.partial(step_kernel, n_grp, n_blk), out_shape=(j...  50.8 us
    unnamed x4, local copies, waits for them, and re-layouts  2.53 us

profile of v5, /device:TPU:0, one launch (start us, length us, event | category | flops | bytes accessed | tf_op | source)
XLA Modules:
  0.0 54.0 jit_solution(11450932730478135636)
XLA Ops:
  0.6 50.8 %step.1 = (f32[8,64,128]{2,1,0:T(8,128)}, f32[128,1024]{1,0:T(8,128)}) custom-call(f32[8,64,128]{2,1,0:T(8,128)} %temp.1, f32[8,64,128]{2,1,0:T(8,128)} %uvel.1, f32[8,64,128]{2,1,0:T(8,128)} %vvel.1, s32[1,2048]{1,0:T(1,128)} %bitcast.3, s32[1,2048]{1,0:T(1,128)} %bitcast.4, s32[1,2048]{1,0:T(1,128)} %bitcast.5, f32[128,1024]{1,0:T(8,128)} %thick.1, ...), custom_call_target="tpu_custom_call" | custom-call | tf_op jit(solution)/shard_map/step/pallas_call | solution.py:547
  51.4 0.0 copy-start
  51.4 1.7 %copy.14 = f32[8,64,128]{2,1,0:T(8,128)} copy(f32[8,64,128]{2,1,0:T(8,128)} %get-tuple-element.4) | data formatting | bytes 524288
  53.2 0.0 copy-done
  53.2 0.8 %copy.15 = f32[128,1024]{1,0:T(8,128)} copy(f32[128,1024]{1,0:T(8,128)S(1)} %copy-done) | data formatting | bytes 1048576
Async XLA Ops:
  51.4 1.7 %copy-start = (f32[128,1024]{1,0:T(8,128)S(1)}, f32[128,1024]{1,0:T(8,128)}, u32[]{:S(2)}) copy-start(f32[128,1024]{1,0:T(8,128)} %get-tuple-element.5) | copy-start | bytes 1572868
